TPU v7x, 128 devices: a whole 4x4x4 slice. The times are simulated.
128 devices in a mesh: row: 8 (over x, core), col: 16 (over y, z).
Axes of the slice: x: 4, y: 4, z: 4, core: 2. Of those that a mesh axis runs over, the one named last changes fastest.
Arguments:
- fields: float32 [5, 96, 512, 1024], P(None, None, 'col', 'row'), may hold values from -6 to 6
- heights: int32 [512, 1024], P('col', 'row'), may hold values from 0 to 24, as said below
- wall_class: int32 [96, 512, 1024], P(None, 'col', 'row'), may hold values from 0 to 3
Outputs:
- new_fields: float32 [5, 96, 512, 1024], P(None, None, 'col', 'row')
- pressure: float32 [96, 512, 1024], P(None, 'col', 'row')
Inputs may be any that keep to these rules, and one draw needn't show every extreme that they name: `heights`: heights are equal within each aligned tile of 8 x 8 columns; some tile has height 24 and some has 0.
All inputs are finite; a program needn't handle non-finite values.
Results may differ from a plain program's by a relative error of at most 0.0003.
Values sent between devices are 32-bit elements; how exact they have to be, the bound alone decides.
No kernel may reach another device: no remote copies, remote signals or barrier semaphores. Data moves between devices by JAX's collectives and lax.ppermute only.
A program may use at most 256 MiB of HBM per device.

v0:
```python
import math

import jax
import jax.numpy as jnp
from jax import lax
from jax.sharding import PartitionSpec as P

spacing = 2.0
step_dt = 0.5
diffusivity = 0.2
drag_table = (0.0, 0.4, 0.8, 1.2)
flux_table = (0.0, 0.3, 0.6, 0.9)
wall_values = (1.0, -0.5)
highest = lax.Precision.HIGHEST


def padded_2(cells, sides, width):
    for axis, dim in sides:
        count = lax.axis_size(axis)
        head = lax.slice_in_dim(cells, 0, width, axis=dim)
        tail = lax.slice_in_dim(cells, cells.shape[dim] - width, cells.shape[dim], axis=dim)
        cells = jnp.concatenate(
            [
                lax.ppermute(tail, axis, [(i, (i + 1) % count) for i in range(count)]),
                cells,
                lax.ppermute(head, axis, [((i + 1) % count, i) for i in range(count)]),
            ],
            axis=dim,
        )
    return cells


def from_behind(value, axis, steps):
    count = lax.axis_size(axis)
    pairs = [(source, (source + steps) % count) for source in range(count)]
    return lax.ppermute(value, axis, pairs)


def lookup(table, wall_class):
    total = jnp.zeros(wall_class.shape, jnp.float32)
    for number in range(4):
        total = total + table[number] * (wall_class == number).astype(jnp.float32)
    return total


def provisional_fields(center, east_side, west_side, north_side, south_side, heights, wall_class):
    upper_side = jnp.concatenate([center[:, 1:], center[:, -1:]], axis=1)
    lower_side = jnp.concatenate([center[:, :1], center[:, :-1]], axis=1)
    velocity_u = center[0]
    velocity_v = center[1]
    velocity_w = center[2]
    advection = (
        velocity_u * (east_side - west_side)
        + velocity_v * (north_side - south_side)
        + velocity_w * (upper_side - lower_side)
    ) / (2.0 * spacing)
    laplacian = (
        east_side + west_side + north_side + south_side + upper_side + lower_side - 6.0 * center
    ) / (spacing * spacing)
    speed_mag = jnp.sqrt(
        velocity_u * velocity_u + velocity_v * velocity_v + velocity_w * velocity_w + 0.01
    )
    drag_coef = lookup(drag_table, wall_class)
    flux_coef = lookup(flux_table, wall_class)
    momentum = -drag_coef * speed_mag * center[:3]
    targets = jnp.array(wall_values, jnp.float32)[:, None, None, None]
    scalar_terms = flux_coef * (targets - center[3:])
    tendency = (
        -advection + diffusivity * laplacian + jnp.concatenate([momentum, scalar_terms], axis=0)
    )
    levels = jnp.arange(center.shape[1], dtype=jnp.int32)[:, None, None]
    fluid_mask = (levels >= heights[None]).astype(jnp.float32)
    velocities = fluid_mask * (center[:3] + step_dt * tendency[:3])
    scalar_new = center[3:] + step_dt * fluid_mask * tendency[3:]
    return (velocities, scalar_new, fluid_mask)


def horizontal_eigen(start_x, count_x, total_x, start_y, count_y, total_y):
    wave_x = (start_x + jnp.arange(count_x, dtype=jnp.int32)).astype(jnp.float32) * (
        2.0 * math.pi / total_x
    )
    wave_y = (start_y + jnp.arange(count_y, dtype=jnp.int32)).astype(jnp.float32) * (
        2.0 * math.pi / total_y
    )
    return (2.0 * jnp.cos(wave_x)[:, None] - 2.0 + 2.0 * jnp.cos(wave_y)[None, :] - 2.0) / (
        spacing * spacing
    )


def tridiagonal(real_src, imag_src, eigen_horiz):
    inverse_sq = 1.0 / (spacing * spacing)
    depth = real_src.shape[0]
    diag_base = jnp.full((depth,), -2.0 * inverse_sq, jnp.float32)
    diag_base = diag_base.at[0].set(-inverse_sq).at[depth - 1].set(-3.0 * inverse_sq)

    def factor_step(factor_prev, base_level):
        denominator = base_level + eigen_horiz - inverse_sq * factor_prev
        factor = inverse_sq / denominator
        return (factor, (factor, denominator))

    unused, (factors, denominators) = lax.scan(
        factor_step, jnp.zeros_like(eigen_horiz), diag_base, unroll=8
    )

    def forward(reduced_prev, inputs):
        real_level, imag_level, denominator = inputs
        real_red = (real_level - inverse_sq * reduced_prev[0]) / denominator
        imag_red = (imag_level - inverse_sq * reduced_prev[1]) / denominator
        return ((real_red, imag_red), (real_red, imag_red))

    initial = (jnp.zeros_like(real_src[0]), jnp.zeros_like(imag_src[0]))
    unused_red, (real_all, imag_all) = lax.scan(
        forward, initial, (real_src, imag_src, denominators), unroll=8
    )

    def backward(above_val, inputs):
        factor, real_red, imag_red = inputs
        current = (real_red - factor * above_val[0], imag_red - factor * above_val[1])
        return (current, current)

    unused_last, (real_out, imag_out) = lax.scan(
        backward, initial, (factors, real_all, imag_all), reverse=True, unroll=8
    )
    return (real_out, imag_out)


def dft_tables(length):
    indices = jnp.arange(length, dtype=jnp.int32)
    products = indices[:, None] * indices[None, :] % length
    angles = products.astype(jnp.float32) * (2.0 * math.pi / length)
    return (jnp.cos(angles), jnp.sin(angles))


def along_last(array, matrix):
    return jnp.einsum("zxn,nk->zxk", array, matrix, precision=highest)


def along_middle(array, matrix):
    return jnp.einsum("znb,nk->zkb", array, matrix, precision=highest)


def forward_real(planes, cosines, sines, apply):
    return (apply(planes, cosines), -apply(planes, sines))


def forward_complex(real_part, imag_part, cosines, sines, apply):
    new_real = apply(real_part, cosines) + apply(imag_part, sines)
    new_imag = apply(imag_part, cosines) - apply(real_part, sines)
    return (new_real, new_imag)


def inverse_complex(real_part, imag_part, cosines, sines, apply):
    length = cosines.shape[0]
    new_real = (apply(real_part, cosines) - apply(imag_part, sines)) / length
    new_imag = (apply(imag_part, cosines) + apply(real_part, sines)) / length
    return (new_real, new_imag)


def inverse_real(real_part, imag_part, cosines, sines, apply):
    length = cosines.shape[0]
    return (apply(real_part, cosines) - apply(imag_part, sines)) / length


def solve_modes(real_part, imag_part):
    count_x = real_part.shape[1]
    count_y = real_part.shape[2]
    eigen_horiz = horizontal_eigen(
        lax.axis_index("row") * count_x,
        count_x,
        count_x * lax.axis_size("row"),
        lax.axis_index("col") * count_y,
        count_y,
        count_y * lax.axis_size("col"),
    )
    return tridiagonal(real_part, imag_part, eigen_horiz)


def on_device(fields, heights, wall_class):
    padded = padded_2(fields, (("row", 3), ("col", 2)), 1)
    center = padded[:, :, 1:-1, 1:-1]
    east_side = padded[:, :, 2:, 1:-1]
    west_side = padded[:, :, :-2, 1:-1]
    north_side = padded[:, :, 1:-1, 2:]
    south_side = padded[:, :, 1:-1, :-2]
    velocities, scalar_new, fluid_mask = provisional_fields(
        center, east_side, west_side, north_side, south_side, heights, wall_class
    )
    prov_u = velocities[0]
    prov_v = velocities[1]
    prov_w = velocities[2]
    u_west = from_behind(prov_u[:, -1:, :], "col", 1)
    v_south = from_behind(prov_v[:, :, -1:], "row", 1)
    u_prev = jnp.concatenate([u_west, prov_u[:, :-1, :]], axis=1)
    v_prev = jnp.concatenate([v_south, prov_v[:, :, :-1]], axis=2)
    w_prev = jnp.concatenate([jnp.zeros_like(prov_w[:1]), prov_w[:-1]], axis=0)
    source = (prov_u - u_prev + (prov_v - v_prev) + (prov_w - w_prev)) / (spacing * step_dt)
    planes = lax.all_to_all(source, "col", split_axis=0, concat_axis=1, tiled=True)
    cos_x, sin_x = dft_tables(planes.shape[1])
    real_part, imag_part = forward_real(planes, cos_x, sin_x, along_middle)
    real_part, imag_part = (
        lax.all_to_all(real_part, "row", split_axis=1, concat_axis=2, tiled=True),
        lax.all_to_all(imag_part, "row", split_axis=1, concat_axis=2, tiled=True),
    )
    cos_y, sin_y = dft_tables(real_part.shape[2])
    real_part, imag_part = forward_complex(real_part, imag_part, cos_y, sin_y, along_last)
    real_part, imag_part = (
        lax.all_to_all(real_part, "col", split_axis=2, concat_axis=0, tiled=True),
        lax.all_to_all(imag_part, "col", split_axis=2, concat_axis=0, tiled=True),
    )
    real_part, imag_part = solve_modes(real_part, imag_part)
    real_part, imag_part = (
        lax.all_to_all(real_part, "col", split_axis=0, concat_axis=2, tiled=True),
        lax.all_to_all(imag_part, "col", split_axis=0, concat_axis=2, tiled=True),
    )
    real_part, imag_part = inverse_complex(real_part, imag_part, cos_y, sin_y, along_last)
    real_part, imag_part = (
        lax.all_to_all(real_part, "row", split_axis=2, concat_axis=1, tiled=True),
        lax.all_to_all(imag_part, "row", split_axis=2, concat_axis=1, tiled=True),
    )
    planes = inverse_real(real_part, imag_part, cos_x, sin_x, along_middle)
    pressure = lax.all_to_all(planes, "col", split_axis=1, concat_axis=0, tiled=True)
    p_east = from_behind(pressure[:, :1, :], "col", -1)
    p_north = from_behind(pressure[:, :, :1], "row", -1)
    grad_x = (jnp.concatenate([pressure[:, 1:, :], p_east], axis=1) - pressure) / spacing
    grad_y = (jnp.concatenate([pressure[:, :, 1:], p_north], axis=2) - pressure) / spacing
    grad_z = jnp.concatenate([pressure[1:] - pressure[:-1], -2.0 * pressure[-1:]], axis=0) / spacing
    corrected = fluid_mask * (velocities - step_dt * jnp.stack([grad_x, grad_y, grad_z], axis=0))
    new_fields = jnp.concatenate([corrected, scalar_new], axis=0)
    return (new_fields, pressure)


def solution(mesh):
    in_specs = (P(None, None, "col", "row"), P("col", "row"), P(None, "col", "row"))
    out_specs = (P(None, None, "col", "row"), P(None, "col", "row"))
    return jax.shard_map(
        on_device, mesh=mesh, in_specs=in_specs, out_specs=out_specs, check_vma=False
    )
```

profile of v0, /device:TPU:1, one launch (start us, length us, event | category | flops | bytes accessed | tf_op | source)
XLA Modules:
  0.0 1207.1 jit_solution(3776729298647620277)
XLA Ops:
  0.6 13.4 %fusion.230 = (f32[5,96,32,1]{3,2,1,0:T(8,128)}, f32[5,96,32,1]{3,2,1,0:T(8,128)}) fusion(f32[5,96,32,128]{3,2,1,0:T(8,128)} %param.14), kind=kLoop, calls=%fused_computation.341 | loop fusion | bytes 245760 | tf_op jit(solution)/shard_map/slice | solution.py:21
  31.6 12.8 %fusion.231 = (f32[5,95,32,128]{3,2,1,0:T(8,128)}, f32[5,95,32,128]{3,2,1,0:T(8,128)}) fusion(f32[5,96,32,128]{3,2,1,0:T(8,128)} %param.14), kind=kLoop, calls=%fused_computation.342 | loop fusion | bytes 31129600 | tf_op jit(solution)/shard_map/slice | solution.py:47
  82.1 8.4 collective-permute-done.2
  95.9 35.6 %maximum_add_fusion = f32[5,96,32,128]{3,2,1,0:T(8,128)} fusion(f32[2,96,32,128]{3,2,1,0:T(8,128)} %subtract_multiply_fusion, f32[3,96,32,128]{3,2,1,0:T(8,128)} %slice_multiply_fusion.1, f32[5,96,32,128]{3,2,1,0:T(8,128)} %param.14, f32[5,95,32,128]{3,2,1,0:T(8,128)} %get-tuple-element.521, f32[5,1,32,128]{3,2,1,0:T(8,128)S(1)} %get-tuple-element.523, ...), kind=kLoop, calls=%fused_computation.192 | loop fusion | flops 60948480 | bytes 44662272 | tf_op jit(solution)/shard_map/add | solution.py:69
  156.5 28.1 %all_to_all.177 = f32[96,32,128]{2,1,0:T(8,128)S(1)} all-to-all(f32[96,32,128]{2,1,0:T(8,128)S(1)} %fusion.112), channel_id=1, replica_groups=mesh['row'=8,'col'=16] {'col'}, dimensions={0} | all-to-all | bytes 3145728 | tf_op jit(solution)/shard_map/all_to_all | solution.py:197
  199.1 8.0 negate_bitcast_fusion
  209.5 16.0 %all-to-all-done.1 = f32[6,512,128]{2,0,1:T(8,128)S(1)} async-done(((f32[6,512,128]{2,0,1:T(8,128)}), f32[6,512,128]{2,0,1:T(8,128)S(1)}, u32[]{:S(2)}, u32[]{:S(2)}) %all-to-all-start.1) | async-done | bytes 1572896 | tf_op jit(solution)/shard_map/all_to_all | solution.py:201
  234.4 21.8 %fusion.85 = f32[6,64,1024]{2,1,0:T(8,128)} fusion(f32[6,64,1024]{2,1,0:T(8,128)S(1)} %all_to_all.135), kind=kOutput, calls=%fused_computation.211 | convolution fusion | flops 4846518272 | bytes 3145728 | tf_op jit(solution)/shard_map/zxn,nk->zxk/dot_general | solution.py:135
  261.1 23.4 %fusion.122 = f32[6,64,1024]{2,1,0:T(8,128)S(1)} fusion(f32[6,64,1024]{2,1,0:T(8,128)} %fusion.85, f32[6,64,1024]{2,1,0:T(8,128)} %all_to_all.139), kind=kOutput, calls=%fused_computation.268 | convolution fusion | flops 4846911488 | bytes 4718592 | tf_op jit(solution)/shard_map/zxn,nk->zxk/dot_general | solution.py:135
  296.4 23.2 %fusion.87 = f32[6,64,1024]{2,1,0:T(8,128)S(1)} fusion(f32[6,64,1024]{2,1,0:T(8,128)} %all_to_all.139), kind=kOutput, calls=%fused_computation.213 | convolution fusion | flops 4846518272 | bytes 3145728 | tf_op jit(solution)/shard_map/zxn,nk->zxk/dot_general | solution.py:135
  319.7 21.7 %fusion.119 = f32[6,64,1024]{2,1,0:T(8,128)} fusion(f32[6,64,1024]{2,1,0:T(8,128)S(1)} %fusion.87, f32[6,64,1024]{2,1,0:T(8,128)S(1)} %all_to_all.135), kind=kOutput, calls=%fused_computation.267 | convolution fusion | flops 4846911488 | bytes 4718592 | tf_op jit(solution)/shard_map/zxn,nk->zxk/dot_general | solution.py:135
  359.6 320.4 %while.56 = (s32[]{:T(128)}, f32[64,64]{1,0:T(8,128)S(1)}, f32[12,8,64,64]{3,2,1,0:T(8,128)}, f32[12,8,64,64]{3,2,1,0:T(8,128)S(1)}, f32[64]{0:T(128)S(1)}, /*in...) while((s32[]{:T(128)}, f32[64,64]{1,0:T(8,128)S(1)}, f32[12,8,64,64]{3,2,1,0:T(8,128)}, ...), condition=%wide.region_1.2_spmd.clone, body=%wide.region_0.1_spmd.clone.sunk | while | flops 716801 | bytes 2026880 | solution.py:101
  680.6 7.0 reduce.5
  717.1 166.6 %while.57 = (s32[]{:T(128)}, f32[64,64]{1,0:T(8,128)S(1)}, f32[64,64]{1,0:T(8,128)}, f32[12,8,64,64]{3,2,1,0:T(8,128)}, f32[12,8,64,64]{3,2,1,0:T(8,128)}, /*ind...) while((s32[]{:T(128)}, f32[64,64]{1,0:T(8,128)S(1)}, ...), condition=%wide.region_3.4_spmd.clone, body=%wide.region_2.3_spmd.clone.sunk | while | flops 204808 | bytes 3395900 | solution.py:112
  886.1 25.0 %while.58 = (s32[]{:T(128)}, f32[64,64]{1,0:T(8,128)S(1)}, f32[64,64]{1,0:T(8,128)S(1)}, f32[12,8,64,64]{3,2,1,0:T(8,128)S(1)}, f32[12,8,64,64]{3,2,1,0:T(8,128)...) while((s32[]{:T(128)}, f32[64,64]{1,0:T(8,128)S(1)}, ...), condition=%wide.region_5.6_spmd.clone, body=%wide.region_4.5_spmd.clone.sunk | while | flops 139273 | bytes 2982195 | solution.py:121
  914.0 7.1 all-to-all-start.5
  924.0 17.5 %all-to-all-done.5 = f32[16,1,24576]{2,1,0:T(1,128)} async-done(((f32[16,1,24576]{2,1,0:T(1,128)}), f32[16,1,24576]{2,1,0:T(1,128)}, u32[]{:S(2)}, u32[]{:S(2)}) %all-to-all-start.5) | async-done | bytes 1572896 | tf_op jit(solution)/shard_map/all_to_all | solution.py:212
  946.2 7.0 reduce.7
  961.9 22.2 %fusion.81 = f32[6,64,1024]{2,1,0:T(8,128)} fusion(f32[6,64,1024]{2,1,0:T(8,128)S(1)} %all_to_all.149), kind=kOutput, calls=%fused_computation.207 | convolution fusion | flops 4846518272 | bytes 3145728 | tf_op jit(solution)/shard_map/zxn,nk->zxk/dot_general | solution.py:135
  1000.1 22.6 %add_multiply_fusion.1 = f32[6,64,1024]{2,1,0:T(8,128)S(1)} fusion(f32[6,64,1024]{2,1,0:T(8,128)} %fusion.81, f32[6,64,1024]{2,1,0:T(8,128)S(1)} %all_to_all.153), kind=kOutput, calls=%fused_computation.249 | convolution fusion | flops 4847304704 | bytes 4718592 | tf_op jit(solution)/shard_map/zxn,nk->zxk/dot_general | solution.py:135
  1032.3 7.9 all-to-all-start.8
  1040.2 21.8 %fusion.83 = f32[6,64,1024]{2,1,0:T(8,128)S(1)} fusion(f32[6,64,1024]{2,1,0:T(8,128)S(1)} %all_to_all.153), kind=kOutput, calls=%fused_computation.209 | convolution fusion | flops 4846518272 | bytes 3145728 | tf_op jit(solution)/shard_map/zxn,nk->zxk/dot_general | solution.py:135
  1062.1 21.7 %subtract_multiply_fusion.1 = f32[6,64,1024]{2,1,0:T(8,128)S(1)} fusion(f32[6,64,1024]{2,1,0:T(8,128)S(1)} %fusion.83, f32[6,64,1024]{2,1,0:T(8,128)S(1)} %copy-done.11), kind=kOutput, calls=%fused_computation.250 | convolution fusion | flops 4847304704 | bytes 4718592 | tf_op jit(solution)/shard_map/zxn,nk->zxk/dot_general | solution.py:135
  1158.5 20.8 %all-to-all-done.9 = f32[6,512,128]{2,0,1:T(8,128)S(1)} async-done(((f32[6,512,128]{2,0,1:T(8,128)}), f32[6,512,128]{2,0,1:T(8,128)S(1)}, u32[]{:S(2)}, u32[]{:S(2)}) %all-to-all-start.9) | async-done | bytes 1572896 | tf_op jit(solution)/shard_map/all_to_all | solution.py:221
  (640 shorter events, 834.9 us)
Async XLA Ops:
  19.3 40.6 %collective-permute-start = (f32[5,96,32,1]{1,2,3,0:T(8,128)S(1)}, f32[5,96,32,1]{1,2,3,0:T(8,128)S(1)}, u32[]{:S(2)}, u32[]{:S(2)}) collective-permute-start(f32[5,96,32,1]{1,2,3,0:T(8,128)S(1)} %copy.123), channel_id=1, source_target_pairs={{0,16},{16,32},{32,48},{48,64},{64,80},{80,96},{96,112},{112,0},{1... | collective-permute-start | bytes 184328 | tf_op jit(solution)/shard_map/ppermute | solution.py:24
  27.0 37.5 %collective-permute-start.1 = (f32[5,96,32,1]{1,2,3,0:T(8,128)S(1)}, f32[5,96,32,1]{1,2,3,0:T(8,128)S(1)}, u32[]{:S(2)}, u32[]{:S(2)}) collective-permute-start(f32[5,96,32,1]{1,2,3,0:T(8,128)S(1)} %copy.124), channel_id=1, source_target_pairs={{16,0},{32,16},{48,32},{64,48},{80,64},{96,80},{112,96},{0,112},{1... | collective-permute-start | bytes 184328 | tf_op jit(solution)/shard_map/ppermute | solution.py:26
  68.9 13.0 %copy-start.15 = (s32[32,128]{1,0:T(8,128)S(1)}, s32[32,128]{1,0:T(8,128)}, u32[]{:S(2)}) copy-start(s32[32,128]{1,0:T(8,128)} %param.15) | copy-start | bytes 49156
  68.9 62.6 %slice-start = ((s8[7864320]{0:T(1024)(128)(4,1)}), s8[4194304]{0:T(1024)(128)(4,1)S(1)}, s32[]{:S(2)}) async-start(s8[7864320]{0:T(1024)(128)(4,1)} %bitcast.686), calls=%async_computation.10 | async-start | bytes 8388608
  75.6 14.9 %collective-permute-start.2 = (f32[5,96,1,130]{3,2,1,0:T(1,128)S(1)}, f32[5,96,1,130]{3,2,1,0:T(1,128)}, u32[]{:S(2)}, u32[]{:S(2)}) collective-permute-start(f32[5,96,1,130]{3,2,1,0:T(1,128)S(1)} %get-tuple-element.514), channel_id=1, source_target_pairs={{1,0},{2,1},{3,2},{4,3},{5,4},{6,5},{7,6},{8,7},{9,8},{10,9},{11,1... | collective-permute-start | bytes 748808 | tf_op jit(solution)/shard_map/ppermute | solution.py:26
  81.9 14.0 %collective-permute-start.3 = (f32[5,96,1,130]{3,2,1,0:T(1,128)S(1)}, f32[5,96,1,130]{3,2,1,0:T(1,128)}, u32[]{:S(2)}, u32[]{:S(2)}) collective-permute-start(f32[5,96,1,130]{3,2,1,0:T(1,128)S(1)} %get-tuple-element.513), channel_id=1, source_target_pairs={{0,1},{1,2},{2,3},{3,4},{4,5},{5,6},{6,7},{7,8},{8,9},{9,10},{10,1... | collective-permute-start | bytes 748808 | tf_op jit(solution)/shard_map/ppermute | solution.py:24
  82.1 49.4 %copy-start.2 = (f32[96,32,128]{2,1,0:T(8,128)}, f32[96,32,128]{2,1,0:T(8,128)S(1)}, u32[]{:S(2)}) copy-start(f32[96,32,128]{2,1,0:T(8,128)S(1)} %fusion.117) | copy-start | bytes 4718596
  95.9 35.7 %slice-start.1 = ((s8[7864320]{0:T(1024)(128)(4,1)}), s8[3670016]{0:T(1024)(128)(4,1)S(1)}, s32[]{:S(2)}) async-start(s8[7864320]{0:T(1024)(128)(4,1)} %bitcast.686), calls=%async_computation.11 | async-start | bytes 7340032
  141.3 7.0 collective-permute-start.5
  145.6 6.3 collective-permute-start.4
  194.7 30.7 %all-to-all-start.1 = ((f32[6,512,128]{2,0,1:T(8,128)}), f32[6,512,128]{2,0,1:T(8,128)S(1)}, u32[]{:S(2)}, u32[]{:S(2)}) async-start(f32[6,512,128]{2,0,1:T(8,128)} %copy.100), calls=%async_computation.1 | async-start | bytes 4194304 | tf_op jit(solution)/shard_map/all_to_all | solution.py:201
  225.5 31.7 %all-to-all-start.2 = ((f32[6,512,128]{2,0,1:T(8,128)}), f32[6,512,128]{2,0,1:T(8,128)}, u32[]{:S(2)}, u32[]{:S(2)}) async-start(f32[6,512,128]{2,0,1:T(8,128)} %copy.102), calls=%async_computation.2 | async-start | bytes 4194304 | tf_op jit(solution)/shard_map/all_to_all | solution.py:202
  292.2 58.0 %all-to-all-start.4 = ((f32[16,1,24576]{2,1,0:T(1,128)}), f32[16,1,24576]{2,1,0:T(1,128)S(1)}, u32[]{:S(2)}, u32[]{:S(2)}) async-start(f32[16,1,24576]{2,1,0:T(1,128)} %reshape.323), calls=%async_computation.4 | async-start | bytes 3145728 | tf_op jit(solution)/shard_map/all_to_all | solution.py:208
  350.2 346.6 %all-to-all-start.3 = ((f32[16,1,24576]{2,1,0:T(1,128)}), f32[16,1,24576]{2,1,0:T(1,128)}, u32[]{:S(2)}, u32[]{:S(2)}) async-start(f32[16,1,24576]{2,1,0:T(1,128)} %reshape.321), calls=%async_computation.3 | async-start | bytes 3145728 | tf_op jit(solution)/shard_map/all_to_all | solution.py:207
  914.0 27.5 %all-to-all-start.5 = ((f32[16,1,24576]{2,1,0:T(1,128)}), f32[16,1,24576]{2,1,0:T(1,128)}, u32[]{:S(2)}, u32[]{:S(2)}) async-start(f32[16,1,24576]{2,1,0:T(1,128)} %reshape.327), calls=%async_computation.5 | async-start | bytes 3145728 | tf_op jit(solution)/shard_map/all_to_all | solution.py:212
  941.5 42.7 %all-to-all-start.6 = ((f32[16,1,24576]{2,1,0:T(1,128)}), f32[16,1,24576]{2,1,0:T(1,128)}, u32[]{:S(2)}, u32[]{:S(2)}) async-start(f32[16,1,24576]{2,1,0:T(1,128)} %reshape.325), calls=%async_computation.6 | async-start | bytes 3145728 | tf_op jit(solution)/shard_map/all_to_all | solution.py:213
  961.9 22.3 %copy-start.10 = (f32[6,64,1024]{2,1,0:T(8,128)}, f32[6,64,1024]{2,1,0:T(8,128)S(1)}, u32[]{:S(2)}) copy-start(f32[6,64,1024]{2,1,0:T(8,128)S(1)} %all_to_all.149) | copy-start | bytes 4718596
  1032.3 61.1 %all-to-all-start.8 = ((f32[8,1,49152]{2,1,0:T(1,128)}), f32[8,1,49152]{2,1,0:T(1,128)S(1)}, u32[]{:S(2)}, u32[]{:S(2)}) async-start(f32[8,1,49152]{2,1,0:T(1,128)} %reshape.331), calls=%async_computation.8 | async-start | bytes 3145728 | tf_op jit(solution)/shard_map/all_to_all | solution.py:218
  1040.2 21.9 %copy-start.11 = (f32[6,64,1024]{2,1,0:T(8,128)S(1)}, f32[6,64,1024]{2,1,0:T(8,128)}, u32[]{:S(2)}) copy-start(f32[6,64,1024]{2,1,0:T(8,128)} %copy-done.10) | copy-start | bytes 4718596
  1093.4 26.0 %all-to-all-start.7 = ((f32[8,1,49152]{2,1,0:T(1,128)}), f32[8,1,49152]{2,1,0:T(1,128)S(1)}, u32[]{:S(2)}, u32[]{:S(2)}) async-start(f32[8,1,49152]{2,1,0:T(1,128)} %reshape.329), calls=%async_computation.7 | async-start | bytes 3145728 | tf_op jit(solution)/shard_map/all_to_all | solution.py:217
  1146.0 33.3 %all-to-all-start.9 = ((f32[6,512,128]{2,0,1:T(8,128)}), f32[6,512,128]{2,0,1:T(8,128)S(1)}, u32[]{:S(2)}, u32[]{:S(2)}) async-start(f32[6,512,128]{2,0,1:T(8,128)} %copy.114), calls=%async_computation.9 | async-start | bytes 4194304 | tf_op jit(solution)/shard_map/all_to_all | solution.py:221
  1182.5 14.0 %copy-start = (f32[16,6,32,128]{3,2,1,0:T(8,128)}, f32[16,6,32,128]{3,2,1,0:T(8,128)S(1)}, u32[]{:S(2)}) copy-start(f32[16,6,32,128]{3,2,1,0:T(8,128)S(1)} %copy.116) | copy-start | bytes 4718596
  1186.8 7.4 collective-permute-start.7
  1191.4 5.1 collective-permute-start.6
  (15 other events, 61.4 us)
where the time goes:
time: 1230 us; the launch traced here: 1210 us
  other arithmetic  575 us (47%)
  local copies, waits for them, and re-layouts  248 us (20%)
  matrix products  206 us (17%)
  waiting for transfers between devices  76.2 us (6%)
  starting transfers between devices  70.3 us (6%)
  blocking collectives  28.1 us (2%)
    while x204, other arithmetic  360 us
    dot_general x8, matrix products, along_last(): return jnp.einsum('zxn,nk->zxk', array, matrix, precision=highest)  179 us
    unnamed x58, local copies, waits for them, and re-layouts  67.7 us
    concatenate x24, other arithmetic, tridiagonal(): lax.scan(factor_step, jnp.zeros_like(eigen_horiz), diag_base, unroll=8)  65.7 us
    dynamic_update_slice x36, local copies, waits for them, and re-layouts, tridiagonal(): lax.scan(factor_step, jnp.zeros_like(eigen_horiz), diag_base, unroll=8)  39.9 us
    add x1, other arithmetic, provisional_fields(): -advection + diffusivity * laplacian  35.6 us
    all_to_all x1, blocking collectives, on_device(): lax.all_to_all(source, 'col', split_axis=0, concat_axis=1, tiled=True)  28.1 us
    dot_general x4, matrix products, along_middle(): return jnp.einsum('znb,nk->zkb', array, matrix, precision=highest)  27.9 us
  transfers between devices with their start and end apart: 17, of which 8 were waited for; matrix products, arithmetic and copies ran while one was open for 49% of the time, Pallas kernels for 0%

commit v1 on v0

v1 whole, which is shorter than its diff:
```python
import functools
import math

import jax
import jax.numpy as jnp
import ml_dtypes
import numpy as np
from jax import lax
from jax.experimental import pallas as pl
from jax.experimental.pallas import tpu as pltpu
from jax.sharding import PartitionSpec as P

NZ, BX, BY = 96, 32, 128
CX, RY = 16, 8
ND = CX * RY
CHUNK = 8
PARTS = NZ // CHUNK
bf16 = jnp.bfloat16
f32 = jnp.float32
VMEM_LIMIT = 56 * 1024 * 1024


def halves(matrix):
    high = matrix.astype(ml_dtypes.bfloat16)
    low = (matrix - high.astype(np.float64)).astype(ml_dtypes.bfloat16)
    return high, low


def right_stack(matrix):
    high, low = halves(matrix)
    return np.block([[high, low], [high, np.zeros_like(low)]])


def left_stack(matrix):
    high, low = halves(matrix)
    return np.block([[high, high], [low, np.zeros_like(low)]])


def wide_stack(matrix):
    high, low = halves(matrix)
    return np.concatenate([high, low], axis=1)


def cas(angle):
    return np.cos(angle) + np.sin(angle)


def block_tables():
    levels = np.arange(NZ) + 0.5
    vertical = np.sqrt(2.0 / NZ) * np.cos(np.pi * np.outer(levels, levels) / NZ)
    waves = np.arange(BY)
    sines = np.sin(np.pi * np.outer(waves, waves) / BY)
    to_waves = sines.copy()
    to_waves[0, 0] = 1.0
    from_waves = sines * (2.0 / BY)
    edge_rows = from_waves.copy()
    from_waves[0, 0] = 1.0
    diagonal = (
        2.0
        + (2.0 - 2.0 * np.cos(np.pi * levels / NZ))[:, None]
        + (2.0 - 2.0 * np.cos(np.pi * waves / BY))[None, :]
    )
    edges = np.zeros((BY, BY))
    edges[:, 0] = edge_rows[:, 1]
    edges[0, 0] = 1.0
    edges[:, BX] = edge_rows[:, BY - 1]
    near = sines[1].copy()
    far = sines[BY - 1].copy()
    return dict(
        vertical=left_stack(vertical),
        vertical_right=right_stack(vertical),
        to_waves=right_stack(to_waves),
        plain_sines=right_stack(sines),
        edge_rows=right_stack(edge_rows),
        from_waves=right_stack(from_waves),
        edges=right_stack(edges),
        diagonal=diagonal.astype(np.float32),
        near_far=np.stack([near, far] + [np.zeros(BY)] * 6).astype(np.float32),
    )


def skeleton_tables():
    total_x, total_y = CX * BX, RY * BY
    grid = np.zeros((RY, CX, CX, RY))
    a0, c = np.arange(CX), np.arange(CX)
    b0, r = np.arange(RY), np.arange(RY)
    part_x = cas(2 * np.pi * np.outer(a0, c) / CX)
    part_y = cas(2 * np.pi * np.outer(b0, r) / RY)
    grid = np.einsum("ac,br->bacr", part_x, part_y)
    mirrored = grid[:, -a0 % CX]
    grid = grid.reshape(ND, ND)
    mirrored = mirrored.reshape(ND, ND)
    j, i = np.arange(BY), np.arange(BX)
    b1, a1 = np.arange(BY), np.arange(BX)
    y_forward, y_inverse = [], []
    for b in range(RY):
        angle = 2 * np.pi * np.outer(j, b + RY * b1) / total_y
        y_forward.append(np.concatenate([np.cos(angle), np.sin(angle)]))
        angle_other = 2 * np.pi * np.outer(j, (-b) % RY + RY * b1) / total_y
        y_inverse.append(np.concatenate([np.cos(angle).T, np.sin(angle_other).T]))
    x_forward, x_inverse = [], []
    for a in range(CX):
        angle = 2 * np.pi * np.outer(i, a + CX * a1) / total_x
        x_forward.append(np.concatenate([np.cos(angle), np.sin(angle)]))
        angle_other = 2 * np.pi * np.outer(i, (-a) % CX + CX * a1) / total_x
        x_inverse.append(np.concatenate([np.cos(angle).T, np.sin(angle_other).T]))

    def lanes(blocks):
        matrix = np.concatenate(blocks)
        out = np.concatenate(halves(matrix), axis=1)
        return np.concatenate([out, np.zeros((out.shape[0], 64), out.dtype)], axis=1)

    lane = np.arange(ND)
    lane_b0, lane_a0 = lane // CX, lane % CX
    wave_x = lane_a0[None, :] + CX * a1[:, None]
    wave_y = lane_b0[None, :] + RY * b1[:, None]
    swap = np.zeros((ND, ND))
    swap[(lane_b0 * CX + (-lane_a0) % CX), lane] = 1.0
    return dict(
        grid=left_stack(grid),
        mirrored=left_stack(mirrored),
        grid_back=left_stack(grid.T / (total_x * total_y)),
        y_forward=np.stack([wide_stack(m) for m in y_forward]),
        y_inverse=np.stack([wide_stack(m) for m in y_inverse]),
        x_forward=lanes(x_forward),
        x_inverse=lanes(x_inverse),
        swap=swap.astype(ml_dtypes.bfloat16),
        eigen_x=(2 - 2 * np.cos(2 * np.pi * wave_x / total_x)).astype(np.float32),
        eigen_y=(2 - 2 * np.cos(2 * np.pi * wave_y / total_y)).astype(np.float32),
    )


def split(values):
    high = values.astype(bf16)
    return high, (values - high.astype(f32)).astype(bf16)


def dot(left, right):
    return jnp.dot(left, right, preferred_element_type=f32)


def times_right(values, stack):
    out = dot(jnp.concatenate(split(values), axis=1), stack)
    half = out.shape[1] // 2
    return out[:, :half] + out[:, half:]


def times_left(stack, values):
    out = dot(stack, jnp.concatenate(split(values), axis=0))
    half = out.shape[0] // 2
    return out[:half] + out[half:]


def lane_index(rows):
    return lax.broadcasted_iota(jnp.int32, (rows, BY), 1)


def row_index(rows):
    return lax.broadcasted_iota(jnp.int32, (rows, BY), 0)


def edge_kernel(field, first_x, last_x, first_y, last_y):
    rows = field.at[0].reshape(NZ * BX, BY)
    first_x[0] = rows[pl.ds(0, NZ, stride=BX), :]
    last_x[0] = rows[pl.ds(BX - 1, NZ, stride=BX), :]
    lane = lane_index(BX)

    def step(level, carry):
        first, last = carry
        turned = pltpu.roll(field[0, level], level, axis=1)
        first = jnp.where(lane == level, turned, first)
        last = jnp.where(lane == lax.rem(level + BY - 1, BY), turned, last)
        return first, last

    zero = jnp.zeros((BX, BY), f32)
    first, last = lax.fori_loop(0, NZ, step, (zero, zero), unroll=4)
    first_y[0] = first
    last_y[0] = last


def block_edges(fields):
    plane = pl.BlockSpec((1, NZ, BY), lambda n: (n, 0, 0))
    packed = pl.BlockSpec((1, BX, BY), lambda n: (n, 0, 0))
    return pl.pallas_call(
        edge_kernel,
        grid=(5,),
        in_specs=[pl.BlockSpec((1, NZ, BX, BY), lambda n: (n, 0, 0, 0))],
        out_specs=[plane, plane, packed, packed],
        out_shape=[jax.ShapeDtypeStruct((5, NZ, BY), f32)] * 2
        + [jax.ShapeDtypeStruct((5, BX, BY), f32)] * 2,
        compiler_params=pltpu.CompilerParams(vmem_limit_bytes=VMEM_LIMIT),
    )(fields)


def eliminate(rhs_of, diagonal, factors, reduced):
    def forward(index, carry):
        factor_prev, reduced_prev = carry
        factor = 1.0 / (diagonal[...] - factor_prev)
        value = factor * (rhs_of(index) + reduced_prev)
        factors[index] = factor
        reduced[index] = value
        return factor, value

    zero = jnp.zeros((NZ, BY), f32)
    lax.fori_loop(0, BX - 1, forward, (zero, zero))

    def backward(step, above):
        index = BX - 2 - step
        value = reduced[index] + factors[index] * above
        reduced[index] = value
        return value

    lax.fori_loop(0, BX - 1, backward, zero)


def source_kernel(
    fields_hbm,
    wall_hbm,
    heights,
    west,
    east,
    south,
    north,
    vertical,
    vertical_right,
    to_waves,
    edge_rows,
    edges,
    diagonal,
    new_hbm,
    waves,
    condensed,
    fields,
    wall,
    new,
    source,
    factors,
    reduced,
    in_sem,
    wall_sem,
    out_sem,
):
    def field_copy(part):
        levels = pl.ds(part * CHUNK, CHUNK)
        return pltpu.make_async_copy(
            fields_hbm.at[:, levels], fields.at[:, levels], in_sem.at[part]
        )

    def wall_copy(part):
        levels = pl.ds(part * CHUNK, CHUNK)
        return pltpu.make_async_copy(wall_hbm.at[levels], wall.at[levels], wall_sem.at[part])

    def new_copy(part):
        levels = pl.ds(part * CHUNK, CHUNK)
        return pltpu.make_async_copy(new.at[:, levels], new_hbm.at[:, levels], out_sem.at[part])

    for part in range(PARTS):
        field_copy(part).start()
        wall_copy(part).start()
    field_copy(0).wait()

    lane = lane_index(BX)
    row = row_index(BX)
    zero = jnp.zeros((BX, BY), f32)

    def level_step(level, carry):
        w_below, v_edge = carry
        below = jnp.maximum(level - 1, 0)
        above = jnp.minimum(level + 1, NZ - 1)
        u, v, w = fields[0, level], fields[1, level], fields[2, level]
        fluid = jnp.where(level >= heights[...], 1.0, 0.0).astype(f32)
        carried = fluid * 0.125
        mixed = fluid * 0.025
        u_part, v_part, w_part = u * carried, v * carried, w * carried
        c_east, c_west = mixed - u_part, mixed + u_part
        c_north, c_south = mixed - v_part, mixed + v_part
        c_up, c_down = mixed - w_part, mixed + w_part
        speed = jnp.sqrt(u * u + v * v + w * w + 0.01)
        classes = wall[level].astype(f32)
        own_velocity = fluid * (0.85 - 0.2 * classes * speed)
        flux = fluid * (0.15 * classes)
        own_scalar = 1.0 - fluid * 0.15 - flux
        results = []
        for number in range(5):
            f = fields[number, level]
            f_east = jnp.where(
                row == BX - 1,
                east[number, pl.ds(level, 1)],
                pltpu.roll(f, BX - 1, axis=0),
            )
            f_west = jnp.where(row == 0, west[number, pl.ds(level, 1)], pltpu.roll(f, 1, axis=0))
            shift_north = lax.rem(BY - 1 - level + BY, BY)
            f_north = jnp.where(
                lane == BY - 1,
                pltpu.roll(north[number], shift_north, axis=1),
                pltpu.roll(f, BY - 1, axis=1),
            )
            shift_south = lax.rem(BY + 1 - level, BY)
            f_south = jnp.where(
                lane == 0,
                pltpu.roll(south[number], shift_south, axis=1),
                pltpu.roll(f, 1, axis=1),
            )
            total = (
                (c_east * f_east + c_west * f_west)
                + (c_north * f_north + c_south * f_south)
                + (c_up * fields[number, above] + c_down * fields[number, below])
            )
            if number < 3:
                total = total + own_velocity * f
            else:
                total = total + own_scalar * f + (1.0 if number == 3 else -0.5) * flux
            new[number, level] = total
            results.append(total)
        u_new, v_new, w_new = results[:3]
        u_behind = jnp.where(row == 0, 0.0, pltpu.roll(u_new, 1, axis=0))
        v_behind = jnp.where(lane == 0, 0.0, pltpu.roll(v_new, 1, axis=1))
        divergence = (u_new - u_behind) + (v_new - v_behind) + (w_new - w_below)
        source[pl.ds(level, BX, stride=NZ), :] = -4.0 * divergence
        source[pl.ds(BX * NZ + level, 1), :] = 4.0 * u_new[BX - 1 :]
        v_edge = jnp.where(lane == level, pltpu.roll(v_new, level + 1, axis=1), v_edge)
        return w_new, v_edge

    def part_step(part, carry):
        @pl.when(part < PARTS - 1)
        def _():
            field_copy(part + 1).wait()

        wall_copy(part).wait()
        carry = lax.fori_loop(part * CHUNK, (part + 1) * CHUNK, level_step, carry)
        new_copy(part).start()
        return carry

    _, v_edge = lax.fori_loop(0, PARTS, part_step, (zero, zero))

    for i in range(1, BX):
        along_y = times_right(source[i * NZ : (i + 1) * NZ, :], to_waves[...])
        waves[i - 1] = times_left(vertical[...], along_y)
    own_x = times_left(vertical[...], source[0:NZ, :])
    next_x = times_left(vertical[...], source[BX * NZ : (BX + 1) * NZ, :])

    eliminate(lambda index: waves[index], diagonal, factors, reduced)

    own_x = own_x + times_right(reduced[0], edge_rows[...])
    next_x = next_x + times_right(reduced[BX - 2], edge_rows[...])
    lane_z = lane_index(NZ)
    next_y = times_right(4.0 * v_edge[:, :NZ], vertical_right[...])
    packed = jnp.concatenate([zero[:, :NZ], next_y, jnp.zeros((2 * BX, NZ), f32)], axis=0).T
    for i in range(1, BX):
        merged = jnp.where(lane_z == 0, waves[i - 1], reduced[i - 1])
        ends = pltpu.roll(times_right(merged, edges[...]), i, axis=1)
        packed = packed + jnp.where((lane_z == i) | (lane_z == BX + i), ends, 0.0)
    condensed[pl.ds(0, NZ, stride=3), :] = own_x
    condensed[pl.ds(1, NZ, stride=3), :] = next_x
    condensed[pl.ds(2, NZ, stride=3), :] = packed
    condensed[3 * NZ :, :] = jnp.zeros((3 * (ND - NZ), BY), f32)

    for part in range(PARTS):
        new_copy(part).wait()


vmem_spec = pl.BlockSpec(memory_space=pltpu.VMEM)
any_spec = pl.BlockSpec(memory_space=pl.ANY)


def condensed_source(fields, wall_class, heights, west, east, south, north, tables):
    return pl.pallas_call(
        source_kernel,
        in_specs=[any_spec, any_spec] + [vmem_spec] * 11,
        out_specs=[any_spec, vmem_spec, vmem_spec],
        out_shape=[
            jax.ShapeDtypeStruct((5, NZ, BX, BY), f32),
            jax.ShapeDtypeStruct((BX - 1, NZ, BY), f32),
            jax.ShapeDtypeStruct((3 * ND, BY), f32),
        ],
        scratch_shapes=[
            pltpu.VMEM((5, NZ, BX, BY), f32),
            pltpu.VMEM((NZ, BX, BY), jnp.int32),
            pltpu.VMEM((5, NZ, BX, BY), f32),
            pltpu.VMEM(((BX + 1) * NZ, BY), f32),
            pltpu.VMEM((BX - 1, NZ, BY), f32),
            pltpu.VMEM((BX - 1, NZ, BY), f32),
            pltpu.SemaphoreType.DMA((PARTS,)),
            pltpu.SemaphoreType.DMA((PARTS,)),
            pltpu.SemaphoreType.DMA((PARTS,)),
        ],
        compiler_params=pltpu.CompilerParams(vmem_limit_bytes=VMEM_LIMIT),
    )(
        fields,
        wall_class,
        heights,
        west,
        east,
        south,
        north,
        tables["vertical"],
        tables["vertical_right"],
        tables["to_waves"],
        tables["edge_rows"],
        tables["edges"],
        tables["diagonal"],
    )


def blockwise(values, stacks):
    parts = []
    for b in range(RY):
        other = (-b) % RY
        pair = jnp.concatenate(
            [values[b * CX : (b + 1) * CX], values[other * CX : (other + 1) * CX]], axis=1
        )
        out = dot(jnp.concatenate(split(pair), axis=0), stacks[b])
        parts.append(out[:CX, :BY] + out[:CX, BY:] + out[CX:, :BY])
    return jnp.concatenate(parts, axis=0)


def per_column(values, mirrored, table):
    pair = values + pltpu.roll(mirrored, BX, axis=1)
    pair = pair + pltpu.roll(pair, 2 * BX, axis=1)
    lane, row = lane_index(ND), row_index(ND)
    mine = lax.rem(row, CX)
    wide = jnp.concatenate(
        [jnp.where(mine == 2 * q + lane // 64, pair, 0.0) for q in range(CX // 2)], axis=1
    )
    out = dot(jnp.concatenate(split(wide), axis=0), table)
    top, bottom = out[:ND], out[ND:]
    out = top + pltpu.roll(top, BY - BX, axis=1) + bottom
    return jnp.where(lane < BX, out, 0.0)


def skeleton_kernel(
    mode_eigen,
    received,
    grid,
    mirrored,
    grid_back,
    y_forward,
    y_inverse,
    x_forward,
    x_inverse,
    swap,
    eigen_x,
    eigen_y,
    answer,
):
    own_x = received[pl.ds(0, ND, stride=3), :]
    next_x = received[pl.ds(1, ND, stride=3), :]
    lines_y = received[pl.ds(2, ND, stride=3), :]
    lane = lane_index(ND)
    lines_x = own_x + pltpu.roll(next_x, RY, axis=0)
    before = pltpu.roll(lines_y, BY - BX, axis=1).reshape(CX, RY, BY)
    before = pltpu.roll(before, 1, axis=1).reshape(ND, BY)
    lines_y = jnp.where(lane < BX, lines_y + before, 0.0)

    both = times_left(grid[...], jnp.concatenate([lines_x, lines_y], axis=1))
    turned = times_left(mirrored[...], lines_y)
    spec_x = blockwise(both[:, :BY], y_forward).T
    spec_y = per_column(both[:, BY:], turned, x_forward[...]).T

    base = eigen_y[...] + mode_eigen[0]
    total_x = jnp.zeros((BY, ND), f32)
    sums = []
    for a in range(BX):
        value = (spec_x + spec_y[a : a + 1]) / (base + eigen_x[a : a + 1])
        total_x = total_x + value
        sums.append(jnp.sum(value, axis=0, keepdims=True))
    total_y = jnp.concatenate(sums, axis=0)
    high, low = split(total_y)
    turned = dot(high, swap[...]) + dot(low, swap[...])
    fill = jnp.zeros((ND - BX, ND), f32)
    total_y = jnp.concatenate([total_y, fill], axis=0).T
    turned = jnp.concatenate([turned, fill], axis=0).T
    lines_x = blockwise(total_x.T, y_inverse)
    lines_y = per_column(total_y, turned, x_inverse[...])
    both = times_left(grid_back[...], jnp.concatenate([lines_x, lines_y], axis=1))
    own_x, own_y = both[:, :BY], both[:, BY:]
    next_x = pltpu.roll(own_x, ND - RY, axis=0)
    next_y = pltpu.roll(own_y.reshape(CX, RY, BY), RY - 1, axis=1).reshape(ND, BY)
    answer[pl.ds(0, ND, stride=3), :] = own_x
    answer[pl.ds(1, ND, stride=3), :] = next_x
    answer[pl.ds(2, ND, stride=3), :] = own_y + pltpu.roll(next_y, BX, axis=1)


def skeleton_solve(received, mode_eigen, tables):
    return pl.pallas_call(
        skeleton_kernel,
        in_specs=[pl.BlockSpec(memory_space=pltpu.SMEM)] + [vmem_spec] * 11,
        out_specs=vmem_spec,
        out_shape=jax.ShapeDtypeStruct((3 * ND, BY), f32),
        compiler_params=pltpu.CompilerParams(vmem_limit_bytes=VMEM_LIMIT),
    )(
        mode_eigen,
        received,
        tables["grid"],
        tables["mirrored"],
        tables["grid_back"],
        tables["y_forward"],
        tables["y_inverse"],
        tables["x_forward"],
        tables["x_inverse"],
        tables["swap"],
        tables["eigen_x"],
        tables["eigen_y"],
    )


def correct_kernel(
    before_hbm,
    waves,
    answer,
    heights,
    vertical,
    vertical_right,
    plain_sines,
    from_waves,
    diagonal,
    near_far,
    new_hbm,
    pressure_hbm,
    velocity,
    planes,
    pressure,
    factors,
    reduced,
    in_sem,
    out_sem,
    pressure_sem,
):
    def in_copy(part):
        levels = pl.ds(part * CHUNK, CHUNK)
        return pltpu.make_async_copy(
            before_hbm.at[pl.ds(0, 3), levels], velocity.at[:, levels], in_sem.at[part]
        )

    def out_copy(part):
        levels = pl.ds(part * CHUNK, CHUNK)
        return pltpu.make_async_copy(
            velocity.at[:, levels], new_hbm.at[pl.ds(0, 3), levels], out_sem.at[part]
        )

    def pressure_copy(part):
        levels = pl.ds(part * CHUNK, CHUNK)
        return pltpu.make_async_copy(
            pressure.at[levels], pressure_hbm.at[levels], pressure_sem.at[part]
        )

    for part in range(PARTS):
        in_copy(part).start()

    own_x = answer[pl.ds(0, NZ, stride=3), :]
    next_x = answer[pl.ds(1, NZ, stride=3), :]
    lines_y = answer[pl.ds(2, NZ, stride=3), :]
    lane_z = lane_index(NZ)
    near, far = near_far[0:1], near_far[1:2]
    for i in range(1, BX):
        rhs = waves[i - 1] + lines_y[:, i : i + 1] * near + lines_y[:, BX + i : BX + i + 1] * far
        if i == 1:
            rhs = rhs + times_right(own_x, plain_sines[...])
        if i == BX - 1:
            rhs = rhs + times_right(next_x, plain_sines[...])
        reduced[i - 1] = rhs
    eliminate(lambda index: reduced[index], diagonal, factors, reduced)

    planes[0:NZ, :] = times_left(vertical[...], own_x)
    planes[BX * NZ : (BX + 1) * NZ, :] = times_left(vertical[...], next_x)
    for i in range(1, BX):
        merged = jnp.where(lane_z == 0, lines_y[:, i : i + 1], reduced[i - 1])
        along_y = times_right(merged, from_waves[...])
        planes[i * NZ : (i + 1) * NZ, :] = times_left(vertical[...], along_y)
    tall = jnp.concatenate([lines_y, jnp.zeros((BY - NZ, BY), f32)], axis=0).T
    north = times_right(tall[BX : 2 * BX, :NZ], vertical_right[...])
    north = jnp.concatenate([north, jnp.zeros((BX, BY - NZ), f32)], axis=1)

    lane = lane_index(BX)

    def level_step(level, here):
        above_level = jnp.minimum(level + 1, NZ - 1)
        above = planes[pl.ds(above_level, BX, stride=NZ), :]
        above = jnp.where(level == NZ - 1, -here, above)
        east = planes[pl.ds(NZ + level, BX, stride=NZ), :]
        shift = lax.rem(BY - 1 - level + BY, BY)
        side = jnp.where(
            lane == BY - 1, pltpu.roll(north, shift, axis=1), pltpu.roll(here, BY - 1, axis=1)
        )
        factor = jnp.where(level >= heights[...], 0.25, 0.0).astype(f32)
        velocity[0, level] = velocity[0, level] - factor * (east - here)
        velocity[1, level] = velocity[1, level] - factor * (side - here)
        velocity[2, level] = velocity[2, level] - factor * (above - here)
        pressure[level] = here
        return above

    def part_step(part, here):
        in_copy(part).wait()
        here = lax.fori_loop(part * CHUNK, (part + 1) * CHUNK, level_step, here)
        out_copy(part).start()
        pressure_copy(part).start()
        return here

    lax.fori_loop(0, PARTS, part_step, planes[pl.ds(0, BX, stride=NZ), :])
    for part in range(PARTS):
        out_copy(part).wait()
        pressure_copy(part).wait()


def corrected(before, waves, answer, heights, tables):
    return pl.pallas_call(
        correct_kernel,
        in_specs=[any_spec] + [vmem_spec] * 9,
        out_specs=[any_spec, any_spec],
        out_shape=[
            jax.ShapeDtypeStruct((5, NZ, BX, BY), f32),
            jax.ShapeDtypeStruct((NZ, BX, BY), f32),
        ],
        scratch_shapes=[
            pltpu.VMEM((3, NZ, BX, BY), f32),
            pltpu.VMEM(((BX + 1) * NZ, BY), f32),
            pltpu.VMEM((NZ, BX, BY), f32),
            pltpu.VMEM((BX - 1, NZ, BY), f32),
            pltpu.VMEM((BX - 1, NZ, BY), f32),
            pltpu.SemaphoreType.DMA((PARTS,)),
            pltpu.SemaphoreType.DMA((PARTS,)),
            pltpu.SemaphoreType.DMA((PARTS,)),
        ],
        input_output_aliases={0: 0},
        compiler_params=pltpu.CompilerParams(vmem_limit_bytes=VMEM_LIMIT),
    )(
        before,
        waves,
        answer,
        heights,
        tables["vertical"],
        tables["vertical_right"],
        tables["plain_sines"],
        tables["from_waves"],
        tables["diagonal"],
        tables["near_far"],
    )


def ring(value, axis, step):
    count = lax.axis_size(axis)
    return lax.ppermute(value, axis, [(n, (n + step) % count) for n in range(count)])


def on_device(fields, heights, wall_class):
    block = {name: jnp.asarray(table) for name, table in block_tables().items()}
    skeleton = {name: jnp.asarray(table) for name, table in skeleton_tables().items()}
    first_x, last_x, first_y, last_y = block_edges(fields)
    west = ring(last_x, "col", 1)
    east = ring(first_x, "col", -1)
    south = ring(last_y, "row", 1)
    north = ring(first_y, "row", -1)
    before, waves, condensed = condensed_source(
        fields, wall_class, heights, west, east, south, north, block
    )
    received = lax.all_to_all(condensed, ("col", "row"), 0, 0, tiled=True)
    mode = lax.axis_index("col") * RY + lax.axis_index("row")
    eigen = 2.0 - 2.0 * np.cos(np.pi * (np.arange(ND) + 0.5) / NZ)
    eigen[NZ:] = 1.0
    mode_eigen = lax.dynamic_slice(jnp.asarray(eigen.astype(np.float32)), (mode,), (1,))
    solved = skeleton_solve(received, mode_eigen, skeleton)
    answer = lax.all_to_all(solved, ("col", "row"), 0, 0, tiled=True)
    return tuple(corrected(before, waves, answer, heights, block))


def solution(mesh):
    in_specs = (P(None, None, "col", "row"), P("col", "row"), P(None, "col", "row"))
    out_specs = (P(None, None, "col", "row"), P(None, "col", "row"))
    return jax.shard_map(
        on_device, mesh=mesh, in_specs=in_specs, out_specs=out_specs, check_vma=False
    )
```

time: 1230 us -> 117 us (0.10); the launches traced: 1210 us -> 117 us
  other arithmetic: 575 us -> 0 us
  local copies, waits for them, and re-layouts: 248 us -> 6.24 us
  matrix products: 206 us -> 0 us
  Pallas kernels: 0 us -> 62.6 us
  waiting for transfers between devices: 76.2 us -> 14.7 us
  starting transfers between devices: 70.3 us -> 17.5 us
  blocking collectives: 28.1 us -> 15.3 us
    while x204 -> x0, other arithmetic: 360 us -> none
    dot_general x12 -> x0, matrix products: 206 us -> none  [the longest x8 179 us: along_last(): return jnp.einsum('zxn,nk->zxk', array, matrix, precision=highest)]
    concatenate x52 -> x0, other arithmetic: 104 us -> none  [the longest x24 65.7 us: tridiagonal(): lax.scan(factor_step, jnp.zeros_like(eigen_horiz), diag_base, unroll=8)]
    unnamed x58 -> x10, local copies, waits for them, and re-layouts: 67.7 us -> 1.4 us
    pallas_call x0 -> x4, Pallas kernels: none -> 62.6 us  [the longest x1 28.1 us: condensed_source(): pl.pallas_call(source_kernel, in_specs=[any_spec, any_spec] + [vmem_spec]...]
    all_to_all x9 -> x1, waiting for transfers between devices: 61.2 us -> 10.3 us  [on_device(): received = lax.all_to_all(condensed, ('col', 'row'), 0, 0, tiled=True)]
    add x4 -> x0, other arithmetic: 46.3 us -> none  [the longest x1 35.6 us: provisional_fields(): -advection + diffusivity * laplacian]
    all_to_all x9 -> x1, starting transfers between devices: 52.5 us -> 8.38 us  [on_device(): received = lax.all_to_all(condensed, ('col', 'row'), 0, 0, tiled=True)]
  transfers between devices with their start and end apart: 17 -> 5, of which waited for: 8 -> 3; matrix products, arithmetic and copies ran while one was open for 49% -> 1% of each run, Pallas kernels for 0% -> 0%
where the time goes in v1:
time: 117 us
  Pallas kernels  62.6 us (54%)
  starting transfers between devices  17.5 us (15%)
  blocking collectives  15.3 us (13%)
  waiting for transfers between devices  14.7 us (13%)
  local copies, waits for them, and re-layouts  6.24 us (5%)
    pallas_call x1, Pallas kernels, condensed_source(): pl.pallas_call(source_kernel, in_specs=[any_spec, any_spec] + [vmem_spec]...  28.1 us
    pallas_call x1, Pallas kernels, corrected(): pl.pallas_call(correct_kernel, in_specs=[any_spec] + [vmem_spec] * 9, out...  16 us
    all_to_all x1, blocking collectives, on_device(): answer = lax.all_to_all(solved, ('col', 'row'), 0, 0, tiled=True)  15.3 us
    pallas_call x1, Pallas kernels, block_edges(): pl.pallas_call(edge_kernel, grid=(5,), in_specs=[pl.BlockSpec((1, NZ, BX,...  13 us
    all_to_all x1, waiting for transfers between devices, on_device(): received = lax.all_to_all(condensed, ('col', 'row'), 0, 0, tiled=True)  10.3 us
    ppermute x4, starting transfers between devices, ring(): lax.ppermute(value, axis, [(n, (n + step) % count) for n in range(count)])  9.17 us
    all_to_all x1, starting transfers between devices, on_device(): received = lax.all_to_all(condensed, ('col', 'row'), 0, 0, tiled=True)  8.38 us
    pallas_call x1, Pallas kernels, skeleton_solve(): pl.pallas_call(skeleton_kernel, in_specs=[pl.BlockSpec(memory_space=pltpu...  5.4 us
  transfers between devices with their start and end apart: 5, of which 3 were waited for; matrix products, arithmetic and copies ran while one was open for 1% of the time, Pallas kernels for 0%

profile of v1, /device:TPU:1, one launch (start us, length us, event | category | flops | bytes accessed | tf_op | source)
XLA Modules:
  0.0 117.1 jit_solution(3707421807561104889)
XLA Ops:
  0.6 0.0 copy-start.4
  0.6 13.0 %shard_map.230 = (f32[5,96,128]{2,1,0:T(8,128)}, f32[5,96,128]{2,1,0:T(8,128)}, f32[5,32,128]{2,1,0:T(8,128)}, f32[5,32,128]{2,1,0:T(8,128)}) custom-call(f32[5,96,32,128]{3,2,1,0:T(8,128)} %fields_hbm.1), custom_call_target="tpu_custom_call" | custom-call | tf_op jit(solution)/shard_map/pallas_call | solution.py:184
  13.7 2.5 %collective-permute-start = (f32[5,96,128]{2,1,0:T(8,128)}, f32[5,96,128]{2,1,0:T(8,128)S(1)}, u32[]{:S(2)}, u32[]{:S(2)}) collective-permute-start(f32[5,96,128]{2,1,0:T(8,128)} %get-tuple-element.9), channel_id=1, source_target_pairs={{0,1},{1,2},{2,3},{3,4},{4,5},{5,6},{6,7},{7,8},{8,9},{9,10},{10,1... | collective-permute-start | bytes 737288 | tf_op jit(solution)/shard_map/ppermute | solution.py:642
  16.1 4.6 %collective-permute-start.1 = (f32[5,96,128]{2,1,0:T(8,128)}, f32[5,96,128]{2,1,0:T(8,128)S(1)}, u32[]{:S(2)}, u32[]{:S(2)}) collective-permute-start(f32[5,96,128]{2,1,0:T(8,128)} %get-tuple-element.10), channel_id=1, source_target_pairs={{0,15},{1,0},{2,1},{3,2},{4,3},{5,4},{6,5},{7,6},{8,7},{9,8},{10,9... | collective-permute-start | bytes 737288 | tf_op jit(solution)/shard_map/ppermute | solution.py:642
  20.8 2.1 %collective-permute-start.2 = (f32[5,32,128]{2,1,0:T(8,128)}, f32[5,32,128]{2,1,0:T(8,128)S(1)}, u32[]{:S(2)}, u32[]{:S(2)}) collective-permute-start(f32[5,32,128]{2,1,0:T(8,128)} %get-tuple-element.11), channel_id=1, source_target_pairs={{0,16},{16,32},{32,48},{48,64},{64,80},{80,96},{96,112},{112,0},{1... | collective-permute-start | bytes 245768 | tf_op jit(solution)/shard_map/ppermute | solution.py:642
  22.8 0.0 collective-permute-start.3
  22.8 1.8 %collective-permute-done.2.south = f32[5,32,128]{2,1,0:T(8,128)S(1)} collective-permute-done((f32[5,32,128]{2,1,0:T(8,128)}, f32[5,32,128]{2,1,0:T(8,128)S(1)}, u32[]{:S(2)}, u32[]{:S(2)}) %collective-permute-start.2) | collective-permute-done | bytes 81952 | tf_op jit(solution)/shard_map/ppermute | solution.py:642
  24.6 2.6 %collective-permute-done.3.north = f32[5,32,128]{2,1,0:T(8,128)S(1)} collective-permute-done((f32[5,32,128]{2,1,0:T(8,128)}, f32[5,32,128]{2,1,0:T(8,128)S(1)}, u32[]{:S(2)}, u32[]{:S(2)}) %collective-permute-start.3) | collective-permute-done | bytes 81952 | tf_op jit(solution)/shard_map/ppermute | solution.py:642
  27.2 0.0 collective-permute-done.west
  27.2 0.0 collective-permute-done.1.east
  27.2 0.6 copy-done.3
  27.8 0.1 copy-done
  27.9 0.7 copy-done.1
  28.6 28.1 %shard_map.231 = (f32[5,96,32,128]{3,2,1,0:T(8,128)}, f32[31,96,128]{2,1,0:T(8,128)}, f32[384,128]{1,0:T(8,128)}) custom-call(f32[5,96,32,128]{3,2,1,0:T(8,128)} %fields_hbm.1, s32[96,32,128]{2,1,0:T(8,128)} %wall_hbm.1, s32[32,128]{1,0:T(8,128)} %heights.3, f32[5,96,128]{2,1,0:T(8,128)} %copy-done, f32[5,96,128]{2,1,0:T(8,128)} %copy-done.1, ...), custom_call_target="tpu_custom_call" | custom-call | tf_op jit(solution)/shard_map/pallas_call | solution.py:367
  56.7 1.7 %all_to_all.14 = f32[128,3,128]{2,1,0:T(4,128)} reshape(f32[384,128]{1,0:T(8,128)} %get-tuple-element.15) | data formatting | bytes 393216 | tf_op jit(solution)/shard_map/all_to_all | solution.py:656
  58.4 8.4 %all-to-all-start = ((f32[128,3,128]{2,1,0:T(4,128)}), f32[128,3,128]{2,1,0:T(4,128)S(1)}, u32[]{:S(2)}, u32[]{:S(2)}) async-start(f32[128,3,128]{2,1,0:T(4,128)} %all_to_all.14), calls=%async_computation | async-start | bytes 524288 | tf_op jit(solution)/shard_map/all_to_all | solution.py:656
  66.8 0.6 dynamic_slice.3.mode_eigen
  67.4 10.3 %all-to-all-done = f32[128,3,128]{2,1,0:T(4,128)S(1)} async-done(((f32[128,3,128]{2,1,0:T(4,128)}), f32[128,3,128]{2,1,0:T(4,128)S(1)}, u32[]{:S(2)}, u32[]{:S(2)}) %all-to-all-start) | async-done | bytes 196640 | tf_op jit(solution)/shard_map/all_to_all | solution.py:656
  77.7 0.8 all_to_all.16.received
  78.5 5.4 %shard_map.232 = f32[384,128]{1,0:T(8,128)} custom-call(f32[1]{0:T(128)} %dynamic_slice.3.mode_eigen, f32[384,128]{1,0:T(8,128)} %all_to_all.16.received, bf16[256,256]{1,0:T(8,128)(2,1)} %constant.64.clone.grid, bf16[256,256]{1,0:T(8,128)(2,1)} %constant.65.clone.mirrored, bf16[256,256]{1,0:T(8,128)(2,1)} %constant.66.clone.grid_back, ...), custom_call_target="tpu_custom_call" | custom-call | tf_op jit(solution)/shard_map/pallas_call | solution.py:485
  83.9 1.0 all_to_all.17
  84.9 15.3 %all_to_all.22 = f32[128,3,128]{2,1,0:T(4,128)S(1)} all-to-all(f32[128,3,128]{2,1,0:T(4,128)S(1)} %all_to_all.17), channel_id=1, replica_groups=mesh['row'=8,'col'=16] {'col','row'}, dimensions={0} | all-to-all | bytes 393216 | tf_op jit(solution)/shard_map/all_to_all | solution.py:662
  100.2 0.8 all_to_all.19.answer
  101.0 16.0 %shard_map.233 = (f32[5,96,32,128]{3,2,1,0:T(8,128)}, f32[96,32,128]{2,1,0:T(8,128)}) custom-call(f32[5,96,32,128]{3,2,1,0:T(8,128)} %get-tuple-element.13.before_hbm, f32[31,96,128]{2,1,0:T(8,128)} %get-tuple-element.14.waves, f32[384,128]{1,0:T(8,128)} %all_to_all.19.answer, s32[32,128]{1,0:T(8,128)} %heights.3, ...), custom_call_target="tpu_custom_call", output_to_operand_aliasing={{0}: (0, {})} | custom-call | tf_op jit(solution)/shard_map/pallas_call | solution.py:606
  (6 shorter events, 0.0 us)
Async XLA Ops:
  0.6 66.2 %copy-start.4 = (f32[128]{0:T(128)S(1)}, f32[128]{0:T(128)}, u32[]{:S(2)}) copy-start(f32[128]{0:T(128)} %constant.74.clone) | copy-start | bytes 1540
  13.7 13.5 %collective-permute-start = (f32[5,96,128]{2,1,0:T(8,128)}, f32[5,96,128]{2,1,0:T(8,128)S(1)}, u32[]{:S(2)}, u32[]{:S(2)}) collective-permute-start(f32[5,96,128]{2,1,0:T(8,128)} %get-tuple-element.9), channel_id=1, source_target_pairs={{0,1},{1,2},{2,3},{3,4},{4,5},{5,6},{6,7},{7,8},{8,9},{9,10},{10,1... | collective-permute-start | bytes 737288 | tf_op jit(solution)/shard_map/ppermute | solution.py:642
  16.1 11.1 %collective-permute-start.1 = (f32[5,96,128]{2,1,0:T(8,128)}, f32[5,96,128]{2,1,0:T(8,128)S(1)}, u32[]{:S(2)}, u32[]{:S(2)}) collective-permute-start(f32[5,96,128]{2,1,0:T(8,128)} %get-tuple-element.10), channel_id=1, source_target_pairs={{0,15},{1,0},{2,1},{3,2},{4,3},{5,4},{6,5},{7,6},{8,7},{9,8},{10,9... | collective-permute-start | bytes 737288 | tf_op jit(solution)/shard_map/ppermute | solution.py:642
  20.8 3.9 %collective-permute-start.2 = (f32[5,32,128]{2,1,0:T(8,128)}, f32[5,32,128]{2,1,0:T(8,128)S(1)}, u32[]{:S(2)}, u32[]{:S(2)}) collective-permute-start(f32[5,32,128]{2,1,0:T(8,128)} %get-tuple-element.11), channel_id=1, source_target_pairs={{0,16},{16,32},{32,48},{48,64},{64,80},{80,96},{96,112},{112,0},{1... | collective-permute-start | bytes 245768 | tf_op jit(solution)/shard_map/ppermute | solution.py:642
  22.8 4.4 %collective-permute-start.3 = (f32[5,32,128]{2,1,0:T(8,128)}, f32[5,32,128]{2,1,0:T(8,128)S(1)}, u32[]{:S(2)}, u32[]{:S(2)}) collective-permute-start(f32[5,32,128]{2,1,0:T(8,128)} %get-tuple-element.12), channel_id=1, source_target_pairs={{0,112},{16,0},{32,16},{48,32},{64,48},{80,64},{96,80},{112,96},{1... | collective-permute-start | bytes 245768 | tf_op jit(solution)/shard_map/ppermute | solution.py:642
  24.6 2.6 %copy-start.2 = (f32[5,32,128]{2,1,0:T(8,128)}, f32[5,32,128]{2,1,0:T(8,128)S(1)}, u32[]{:S(2)}) copy-start(f32[5,32,128]{2,1,0:T(8,128)S(1)} %collective-permute-done.2.south) | copy-start | bytes 245764
  27.2 0.6 copy-start.3
  27.2 0.7 copy-start
  27.9 0.7 copy-start.1
  58.4 19.3 %all-to-all-start = ((f32[128,3,128]{2,1,0:T(4,128)}), f32[128,3,128]{2,1,0:T(4,128)S(1)}, u32[]{:S(2)}, u32[]{:S(2)}) async-start(f32[128,3,128]{2,1,0:T(4,128)} %all_to_all.14), calls=%async_computation | async-start | bytes 524288 | tf_op jit(solution)/shard_map/all_to_all | solution.py:656

commit v2 on v1

v2 whole, which is shorter than its diff:
```python
import functools
import math

import jax
import jax.numpy as jnp
import ml_dtypes
import numpy as np
from jax import lax
from jax.experimental import pallas as pl
from jax.experimental.pallas import tpu as pltpu
from jax.sharding import PartitionSpec as P

NZ, BX, BY = 96, 32, 128
CX, RY = 16, 8
ND = CX * RY
CHUNK = 8
ROWS = BX + 16
TALL = BX + 8
PARTS = NZ // CHUNK
bf16 = jnp.bfloat16
f32 = jnp.float32
GRANT = 64 * 1024 * 1024


def halves(matrix):
    high = matrix.astype(ml_dtypes.bfloat16)
    low = (matrix - high.astype(np.float64)).astype(ml_dtypes.bfloat16)
    return high, low


def right_stack(matrix):
    high, low = halves(matrix)
    return np.block([[high, low], [high, np.zeros_like(low)]])


def left_stack(matrix):
    high, low = halves(matrix)
    return np.block([[high, high], [low, np.zeros_like(low)]])


def wide_stack(matrix):
    high, low = halves(matrix)
    return np.concatenate([high, low], axis=1)


def cas(angle):
    return np.cos(angle) + np.sin(angle)


def block_tables():
    levels = np.arange(NZ) + 0.5
    vertical = np.sqrt(2.0 / NZ) * np.cos(np.pi * np.outer(levels, levels) / NZ)
    waves = np.arange(BY)
    sines = np.sin(np.pi * np.outer(waves, waves) / BY)
    to_waves = sines.copy()
    to_waves[0, 0] = 1.0
    from_waves = sines * (2.0 / BY)
    edge_rows = from_waves.copy()
    from_waves[0, 0] = 1.0
    diagonal = (
        2.0
        + (2.0 - 2.0 * np.cos(np.pi * levels / NZ))[:, None]
        + (2.0 - 2.0 * np.cos(np.pi * waves / BY))[None, :]
    )
    factors = [np.zeros((NZ, BY))]
    for _ in range(1, BX):
        factors.append(1.0 / (diagonal - factors[-1]))
    edges = np.zeros((BY, BY))
    edges[:, 0] = edge_rows[:, 1]
    edges[0, 0] = 1.0
    edges[:, BX] = edge_rows[:, BY - 1]
    near = sines[1].copy()
    far = sines[BY - 1].copy()
    return dict(
        vertical=left_stack(vertical),
        vertical_right=right_stack(vertical),
        to_waves=right_stack(to_waves),
        plain_sines=right_stack(sines),
        edge_rows=right_stack(edge_rows),
        from_waves=right_stack(from_waves),
        edges=right_stack(edges),
        factors=np.stack(factors[1:]).astype(np.float32),
        near_far=np.stack([near, far] + [np.zeros(BY)] * 6).astype(np.float32),
    )


def skeleton_tables():
    total_x, total_y = CX * BX, RY * BY
    grid = np.zeros((RY, CX, CX, RY))
    a0, c = np.arange(CX), np.arange(CX)
    b0, r = np.arange(RY), np.arange(RY)
    part_x = cas(2 * np.pi * np.outer(a0, c) / CX)
    part_y = cas(2 * np.pi * np.outer(b0, r) / RY)
    grid = np.einsum("ac,br->bacr", part_x, part_y)
    mirrored = grid[:, -a0 % CX]
    grid = grid.reshape(ND, ND)
    mirrored = mirrored.reshape(ND, ND)
    j, i = np.arange(BY), np.arange(BX)
    b1, a1 = np.arange(BY), np.arange(BX)
    y_forward, y_inverse = [], []
    for b in range(RY):
        angle = 2 * np.pi * np.outer(j, b + RY * b1) / total_y
        y_forward.append(np.concatenate([np.cos(angle), np.sin(angle)]))
        angle_other = 2 * np.pi * np.outer(j, (-b) % RY + RY * b1) / total_y
        y_inverse.append(np.concatenate([np.cos(angle).T, np.sin(angle_other).T]))
    x_forward, x_inverse = [], []
    for a in range(CX):
        angle = 2 * np.pi * np.outer(i, a + CX * a1) / total_x
        x_forward.append(np.concatenate([np.cos(angle), np.sin(angle)]))
        angle_other = 2 * np.pi * np.outer(i, (-a) % CX + CX * a1) / total_x
        x_inverse.append(np.concatenate([np.cos(angle).T, np.sin(angle_other).T]))

    def lanes(blocks):
        matrix = np.concatenate(blocks)
        out = np.concatenate(halves(matrix), axis=1)
        return np.concatenate([out, np.zeros((out.shape[0], 64), out.dtype)], axis=1)

    lane = np.arange(ND)
    lane_b0, lane_a0 = lane // CX, lane % CX
    wave_x = lane_a0[None, :] + CX * a1[:, None]
    wave_y = lane_b0[None, :] + RY * b1[:, None]
    swap = np.zeros((ND, ND))
    swap[(lane_b0 * CX + (-lane_a0) % CX), lane] = 1.0
    return dict(
        grid=left_stack(grid),
        mirrored=left_stack(mirrored),
        grid_back=left_stack(grid.T / (total_x * total_y)),
        y_forward=np.stack([wide_stack(m) for m in y_forward]),
        y_inverse=np.stack([wide_stack(m) for m in y_inverse]),
        x_forward=lanes(x_forward),
        x_inverse=lanes(x_inverse),
        swap=swap.astype(ml_dtypes.bfloat16),
        eigen_x=(2 - 2 * np.cos(2 * np.pi * wave_x / total_x)).astype(np.float32),
        eigen_y=(2 - 2 * np.cos(2 * np.pi * wave_y / total_y)).astype(np.float32),
    )


def split(values):
    high = values.astype(bf16)
    return high, (values - high.astype(f32)).astype(bf16)


def dot(left, right):
    return jnp.dot(left, right, preferred_element_type=f32)


def times_right(values, stack):
    out = dot(jnp.concatenate(split(values), axis=1), stack)
    half = out.shape[1] // 2
    return out[:, :half] + out[:, half:]


def times_left(stack, values):
    out = dot(stack, jnp.concatenate(split(values), axis=0))
    half = out.shape[0] // 2
    return out[:half] + out[half:]


def lane_index(rows):
    return lax.broadcasted_iota(jnp.int32, (rows, BY), 1)


def row_index(rows):
    return lax.broadcasted_iota(jnp.int32, (rows, BY), 0)


def edge_kernel(fields, first_x, last_x, first_y, last_y, held, west, east, south, north, *sems):
    sem, out_sem = sems

    def copy(number):
        return pltpu.make_async_copy(fields.at[number], held.at[number], sem.at[number])

    for number in range(5):
        copy(number).start()
    lane = lane_index(BX)

    def step(number, carry):
        copy(number).wait()
        rows = held.at[number].reshape(NZ * BX, BY)
        east[pl.ds(pl.multiple_of(number * NZ, NZ), NZ), :] = rows[pl.ds(0, NZ, stride=BX), :]
        west[pl.ds(pl.multiple_of(number * NZ, NZ), NZ), :] = rows[pl.ds(BX - 1, NZ, stride=BX), :]
        for group in range(2):
            first, last = jnp.zeros((BX, BY), f32), jnp.zeros((BX, BY), f32)
            for level in range(NZ // 2):
                turned = held[number, group * (NZ // 2) + level]
                if level:
                    turned = pltpu.roll(turned, 2 * level, axis=1)
                first = jnp.where(lane == 2 * level, turned, first)
                last = jnp.where(lane == (2 * level - 1) % BY, turned, last)
            north[2 * number + group] = first
            south[2 * number + group] = last
        return carry

    lax.fori_loop(0, 5, step, 0)
    for copied in fetches(
        [east, west, north, south], [first_x, last_x, first_y, last_y], out_sem
    ):
        copied.wait()


def block_edges(fields):
    plane = (5 * NZ, BY)
    packed = (10, BX, BY)
    shapes = [plane, plane, packed, packed]
    return pl.pallas_call(
        edge_kernel,
        in_specs=[any_spec],
        out_specs=[any_spec] * 4,
        out_shape=[jax.ShapeDtypeStruct(shape, f32) for shape in shapes],
        scratch_shapes=[pltpu.VMEM((5, NZ, BX, BY), f32)]
        + [pltpu.VMEM(shape, f32) for shape in shapes]
        + [pltpu.SemaphoreType.DMA((5,)), pltpu.SemaphoreType.DMA((4,))],
        compiler_params=pltpu.CompilerParams(vmem_limit_bytes=GRANT),
    )(fields)


def eliminate(rhs, factors, reduced):
    def forward(index, reduced_prev):
        value = factors[index] * (rhs[index] + reduced_prev)
        reduced[index] = value
        return value

    zero = jnp.zeros((NZ, BY), f32)
    lax.fori_loop(0, BX - 1, forward, zero, unroll=True)

    def backward(step, above):
        index = BX - 2 - step
        value = reduced[index] + factors[index] * above
        reduced[index] = value
        return value

    lax.fori_loop(0, BX - 1, backward, zero, unroll=True)


def fetches(sources, targets, sem):
    copies = [
        pltpu.make_async_copy(source, target, sem.at[number])
        for number, (source, target) in enumerate(zip(sources, targets))
    ]
    for copy in copies:
        copy.start()
    return copies


def shapes_of(arrays):
    return [pltpu.VMEM(array.shape, array.dtype) for array in arrays]


def part_copy(source, target, sem, part):
    levels = pl.ds(part * CHUNK, CHUNK)
    pick = lambda ref: ref.at[levels] if len(ref.shape) == 3 else ref.at[:, levels]
    return pltpu.make_async_copy(pick(source), pick(target), sem.at[part])


def coefficients(u, v, w, fluid):
    carried = fluid * 0.125
    mixed = fluid * 0.025
    u_part, v_part, w_part = u * carried, v * carried, w * carried
    return (
        mixed - u_part,
        mixed + u_part,
        mixed - v_part,
        mixed + v_part,
        mixed - w_part,
        mixed + w_part,
    )


def aligned(packed, part, offset):
    return pltpu.roll(packed, lax.rem(offset + 2 * BY - part * CHUNK, BY), axis=1)


def turned_back(value, sub):
    return pltpu.roll(value, BY - sub, axis=1) if sub else value


def merged_sides(south, north, sides, numbers):
    even = lax.rem(lane_index(BX), 2) == 0
    for number in numbers:
        for index in (2 * number, 2 * number + 1):
            sides[index] = jnp.where(
                even,
                pltpu.roll(south[index], 1, axis=1),
                pltpu.roll(north[index], BY - 1, axis=1),
            )


def part_sides(sides, number, part):
    group = part // (PARTS // 2)
    start = 2 * CHUNK * lax.rem(part, PARTS // 2)
    return pltpu.roll(sides[2 * number + group], lax.rem(BY - start, BY), axis=1)


def neighbour_sum(ref, n, level, sub, f, up, down, side, coefs, lane):
    c_east, c_west, c_north, c_south, c_up, c_down = coefs
    f_west = ref[n, level, 7 : 7 + BX]
    f_east = ref[n, level, 9 : 9 + BX]
    side = turned_back(side, 2 * sub)
    f_north = jnp.where(lane == BY - 1, side, pltpu.roll(f, BY - 1, axis=1))
    f_south = jnp.where(lane == 0, side, pltpu.roll(f, 1, axis=1))
    return (
        (c_east * f_east + c_west * f_west)
        + (c_north * f_north + c_south * f_south)
        + (c_up * up + c_down * down)
    )


def put_rows(fields, west, east, numbers):
    for slot, number in enumerate(numbers):
        rows = fields.at[slot].reshape(NZ * ROWS, BY)
        rows[pl.ds(7, NZ, stride=ROWS), :] = west[number * NZ : (number + 1) * NZ, :]
        rows[pl.ds(8 + BX, NZ, stride=ROWS), :] = east[number * NZ : (number + 1) * NZ, :]


def near_levels(level, sub):
    below = jnp.maximum(level - 1, 0) if sub == 0 else level - 1
    above = jnp.minimum(level + 1, NZ - 1) if sub == CHUNK - 1 else level + 1
    return below, above


def source_kernel(*refs):
    fields_hbm, wall_hbm = refs[:2]
    inputs, refs = refs[2:13], refs[13:]
    new_hbm, waves_hbm, condensed_hbm = refs[:3]
    held, refs = refs[3:14], refs[14:]
    heights, west, east, south, north = held[:5]
    vertical, vertical_right, to_waves, edge_rows, edges, factors = held[5:]
    fields, wall, new, source, waves, reduced, condensed, sides = refs[:8]
    in_sem, wall_sem, out_sem, held_sem, last_sem = refs[8:]
    copies = fetches(inputs[:5], held[:5], held_sem)

    def field_copy(part):
        levels = pl.ds(part * CHUNK, CHUNK)
        return pltpu.make_async_copy(
            fields_hbm.at[pl.ds(0, 3), levels],
            fields.at[:, levels, pl.ds(8, BX)],
            in_sem.at[part],
        )

    for part in range(PARTS):
        field_copy(part).start()
        part_copy(wall_hbm, wall, wall_sem, part).start()
    tables = fetches(inputs[5:], held[5:], held_sem.at[pl.ds(5, 6)])
    for copy in copies:
        copy.wait()
    put_rows(fields, west, east, range(3))
    merged_sides(south, north, sides, range(3))
    field_copy(0).wait()

    lane = lane_index(BX)
    row = row_index(BX)
    zero = jnp.zeros((BX, BY), f32)

    def part_step(part, carry):
        @pl.when(part < PARTS - 1)
        def _():
            field_copy(part + 1).wait()

        part_copy(wall_hbm, wall, wall_sem, part).wait()
        w_below, v_edge = carry
        turned = [part_sides(sides, n, part) for n in range(3)]
        ends = zero
        for sub in range(CHUNK):
            level = part * CHUNK + sub
            below, above = near_levels(level, sub)
            u, v, w = [fields[n, level, 8 : 8 + BX] for n in range(3)]
            fluid = jnp.where(level >= heights[...], 1.0, 0.0).astype(f32)
            coefs = coefficients(u, v, w, fluid)
            speed = jnp.sqrt(u * u + v * v + w * w + 0.01)
            own = fluid * (0.85 - 0.2 * wall[level].astype(f32) * speed)
            results = []
            for n, f in enumerate((u, v, w)):
                total = own * f + neighbour_sum(
                    fields,
                    n,
                    level,
                    sub,
                    f,
                    fields[n, above, 8 : 8 + BX],
                    fields[n, below, 8 : 8 + BX],
                    turned[n],
                    coefs,
                    lane,
                )
                new[n, level] = total
                results.append(total)
            u_new, v_new, w_new = results
            u_behind = jnp.where(row == 0, 0.0, pltpu.roll(u_new, 1, axis=0))
            v_behind = pltpu.roll(v_new, 1, axis=1)
            ends = jnp.where(lane == sub, turned_back(v_behind, BY - sub), ends)
            v_behind = jnp.where(lane == 0, 0.0, v_behind)
            divergence = (u_new - u_behind) + (v_new - v_behind) + (w_new - w_below)
            source[pl.ds(level, BX, stride=NZ), :] = -4.0 * divergence
            source[pl.ds(BX * NZ + level, 1), :] = 4.0 * u_new[BX - 1 :]
            w_below = w_new
        v_edge = v_edge + pltpu.roll(ends, part * CHUNK, axis=1)
        part_copy(new, new_hbm, out_sem, part).start()
        return w_below, v_edge

    _, v_edge = lax.fori_loop(0, PARTS, part_step, (zero, zero))

    for copy in tables:
        copy.wait()
    for i in range(1, BX):
        along_y = times_right(source[i * NZ : (i + 1) * NZ, :], to_waves[...])
        waves[i - 1] = times_left(vertical[...], along_y)
    own_x = times_left(vertical[...], source[0:NZ, :])
    next_x = times_left(vertical[...], source[BX * NZ : (BX + 1) * NZ, :])

    waves_copy = pltpu.make_async_copy(waves, waves_hbm, last_sem.at[0])
    waves_copy.start()
    eliminate(waves, factors, reduced)

    own_x = own_x + times_right(reduced[0], edge_rows[...])
    next_x = next_x + times_right(reduced[BX - 2], edge_rows[...])
    lane_z = lane_index(NZ)
    next_y = times_right(4.0 * v_edge[:, :NZ], vertical_right[...])
    packed = jnp.concatenate([zero[:, :NZ], next_y, jnp.zeros((2 * BX, NZ), f32)], axis=0).T
    for i in range(1, BX):
        merged = jnp.where(lane_z == 0, waves[i - 1], reduced[i - 1])
        ends = pltpu.roll(times_right(merged, edges[...]), i, axis=1)
        packed = packed + jnp.where((lane_z == i) | (lane_z == BX + i), ends, 0.0)
    condensed[pl.ds(0, NZ, stride=4), :] = own_x
    condensed[pl.ds(1, NZ, stride=4), :] = next_x
    condensed[pl.ds(2, NZ, stride=4), :] = packed
    condensed[pl.ds(3, NZ, stride=4), :] = jnp.zeros((NZ, BY), f32)
    condensed[4 * NZ :, :] = jnp.zeros((4 * (ND - NZ), BY), f32)
    condensed_copy = pltpu.make_async_copy(condensed, condensed_hbm, last_sem.at[1])
    condensed_copy.start()
    waves_copy.wait()
    condensed_copy.wait()
    for part in range(PARTS):
        part_copy(new, new_hbm, out_sem, part).wait()


vmem_spec = pl.BlockSpec(memory_space=pltpu.VMEM)
any_spec = pl.BlockSpec(memory_space=pl.ANY)


def condensed_source(fields, wall_class, heights, west, east, south, north, tables):
    names = ("vertical", "vertical_right", "to_waves", "edge_rows", "edges", "factors")
    held = [heights, west, east, south, north] + [tables[name] for name in names]
    return pl.pallas_call(
        source_kernel,
        in_specs=[any_spec] * 13,
        out_specs=[any_spec] * 3,
        out_shape=[
            jax.ShapeDtypeStruct((3, NZ, BX, BY), f32),
            jax.ShapeDtypeStruct((BX - 1, NZ, BY), f32),
            jax.ShapeDtypeStruct((4 * ND, BY), f32),
        ],
        scratch_shapes=shapes_of(held)
        + [
            pltpu.VMEM((3, NZ, ROWS, BY), f32),
            pltpu.VMEM((NZ, BX, BY), jnp.int32),
            pltpu.VMEM((3, NZ, BX, BY), f32),
            pltpu.VMEM(((BX + 1) * NZ, BY), f32),
            pltpu.VMEM((BX - 1, NZ, BY), f32),
            pltpu.VMEM((BX - 1, NZ, BY), f32),
            pltpu.VMEM((4 * ND, BY), f32),
            pltpu.VMEM((10, BX, BY), f32),
            pltpu.SemaphoreType.DMA((PARTS,)),
            pltpu.SemaphoreType.DMA((PARTS,)),
            pltpu.SemaphoreType.DMA((PARTS,)),
            pltpu.SemaphoreType.DMA((11,)),
            pltpu.SemaphoreType.DMA((2,)),
        ],
        compiler_params=pltpu.CompilerParams(vmem_limit_bytes=GRANT),
        cost_estimate=pl.CostEstimate(flops=0, bytes_accessed=40000000, transcendentals=0),
    )(fields, wall_class, *held)


def scalar_kernel(*refs):
    fields_hbm, wall_hbm = refs[:2]
    inputs, new_hbm, held, refs = refs[2:7], refs[7], refs[8:13], refs[13:]
    heights, west, east, south, north = held
    fields, scalars, wall, new, sides = refs[:5]
    in_sem, scalar_sem, wall_sem, out_sem, held_sem = refs[5:]
    copies = fetches(inputs, held, held_sem)

    def out_copy(part):
        levels = pl.ds(part * CHUNK, CHUNK)
        return pltpu.make_async_copy(
            new.at[:, levels], new_hbm.at[pl.ds(3, 2), levels], out_sem.at[part]
        )

    def in_copy(part):
        levels = pl.ds(part * CHUNK, CHUNK)
        return pltpu.make_async_copy(
            fields_hbm.at[pl.ds(0, 3), levels], fields.at[:, levels], in_sem.at[part]
        )

    def scalar_copy(part):
        levels = pl.ds(part * CHUNK, CHUNK)
        return pltpu.make_async_copy(
            fields_hbm.at[pl.ds(3, 2), levels],
            scalars.at[:, levels, pl.ds(8, BX)],
            scalar_sem.at[part],
        )

    for part in range(PARTS):
        in_copy(part).start()
        scalar_copy(part).start()
        part_copy(wall_hbm, wall, wall_sem, part).start()
    for copy in copies:
        copy.wait()
    put_rows(scalars, west, east, (3, 4))
    merged_sides(south, north, sides, (3, 4))
    scalar_copy(0).wait()
    lane = lane_index(BX)

    def part_step(part, carry):
        @pl.when(part < PARTS - 1)
        def _():
            scalar_copy(part + 1).wait()

        in_copy(part).wait()
        part_copy(wall_hbm, wall, wall_sem, part).wait()
        turned = [part_sides(sides, 3 + n, part) for n in range(2)]
        for sub in range(CHUNK):
            level = part * CHUNK + sub
            below, above = near_levels(level, sub)
            fluid = jnp.where(level >= heights[...], 1.0, 0.0).astype(f32)
            coefs = coefficients(fields[0, level], fields[1, level], fields[2, level], fluid)
            flux = fluid * (0.15 * wall[level].astype(f32))
            own = 1.0 - fluid * 0.15 - flux
            for n, target in enumerate((1.0, -0.5)):
                f = scalars[n, level, 8 : 8 + BX]
                new[n, level] = (own * f + target * flux) + neighbour_sum(
                    scalars,
                    n,
                    level,
                    sub,
                    f,
                    scalars[n, above, 8 : 8 + BX],
                    scalars[n, below, 8 : 8 + BX],
                    turned[n],
                    coefs,
                    lane,
                )
        out_copy(part).start()
        return carry

    lax.fori_loop(0, PARTS, part_step, 0)
    for part in range(PARTS):
        out_copy(part).wait()


def new_scalars(fields, wall_class, *held):
    return pl.pallas_call(
        scalar_kernel,
        in_specs=[any_spec] * 7,
        out_specs=any_spec,
        out_shape=jax.ShapeDtypeStruct((5, NZ, BX, BY), f32),
        scratch_shapes=shapes_of(held)
        + [
            pltpu.VMEM((3, NZ, BX, BY), f32),
            pltpu.VMEM((2, NZ, ROWS, BY), f32),
            pltpu.VMEM((NZ, BX, BY), jnp.int32),
            pltpu.VMEM((2, NZ, BX, BY), f32),
            pltpu.VMEM((10, BX, BY), f32),
            pltpu.SemaphoreType.DMA((PARTS,)),
            pltpu.SemaphoreType.DMA((PARTS,)),
            pltpu.SemaphoreType.DMA((PARTS,)),
            pltpu.SemaphoreType.DMA((PARTS,)),
            pltpu.SemaphoreType.DMA((5,)),
        ],
        compiler_params=pltpu.CompilerParams(vmem_limit_bytes=GRANT),
        cost_estimate=pl.CostEstimate(flops=0, bytes_accessed=30000000, transcendentals=0),
    )(fields, wall_class, *held)


def blockwise(values, stacks):
    parts = []
    for b in range(RY):
        other = (-b) % RY
        pair = jnp.concatenate(
            [values[b * CX : (b + 1) * CX], values[other * CX : (other + 1) * CX]], axis=1
        )
        out = dot(jnp.concatenate(split(pair), axis=0), stacks[b])
        parts.append(out[:CX, :BY] + out[:CX, BY:] + out[CX:, :BY])
    return jnp.concatenate(parts, axis=0)


def per_column(values, mirrored, table):
    pair = values + pltpu.roll(mirrored, BX, axis=1)
    pair = pair + pltpu.roll(pair, 2 * BX, axis=1)
    lane, row = lane_index(ND), row_index(ND)
    mine = lax.rem(row, CX)
    wide = jnp.concatenate(
        [jnp.where(mine == 2 * q + lane // 64, pair, 0.0) for q in range(CX // 2)], axis=1
    )
    out = dot(jnp.concatenate(split(wide), axis=0), table)
    top, bottom = out[:ND], out[ND:]
    out = top + pltpu.roll(top, BY - BX, axis=1) + bottom
    return jnp.where(lane < BX, out, 0.0)


skeleton_names = (
    "grid",
    "mirrored",
    "y_forward",
    "x_forward",
    "eigen_x",
    "eigen_y",
    "swap",
    "y_inverse",
    "x_inverse",
    "grid_back",
)


def skeleton_kernel(mode_eigen, *refs):
    inputs, answer_hbm, held, refs = refs[:11], refs[11], refs[12:23], refs[23:]
    received, grid, mirrored, y_forward, x_forward, eigen_x, eigen_y = held[:7]
    swap, y_inverse, x_inverse, grid_back = held[7:]
    answer, held_sem, last_sem = refs
    copies = fetches(inputs, held, held_sem)
    def wait(first, last):
        for copy in copies[first:last]:
            copy.wait()

    wait(0, 3)
    own_x = received[pl.ds(0, ND, stride=4), :]
    next_x = received[pl.ds(1, ND, stride=4), :]
    lines_y = received[pl.ds(2, ND, stride=4), :]
    lane = lane_index(ND)
    lines_x = own_x + pltpu.roll(next_x, RY, axis=0)
    before = pltpu.roll(lines_y, BY - BX, axis=1).reshape(CX, RY, BY)
    before = pltpu.roll(before, 1, axis=1).reshape(ND, BY)
    lines_y = jnp.where(lane < BX, lines_y + before, 0.0)

    both = times_left(grid[...], jnp.concatenate([lines_x, lines_y], axis=1))
    turned = times_left(mirrored[...], lines_y)
    wait(3, 4)
    spec_x = blockwise(both[:, :BY], y_forward).T
    wait(4, 7)
    spec_y = per_column(both[:, BY:], turned, x_forward[...]).T

    base = eigen_y[...] + mode_eigen[0]
    total_x = jnp.zeros((BY, ND), f32)
    sums = []
    for a in range(BX):
        value = (spec_x + spec_y[a : a + 1]) / (base + eigen_x[a : a + 1])
        total_x = total_x + value
        sums.append(jnp.sum(value, axis=0, keepdims=True))
    total_y = jnp.concatenate(sums, axis=0)
    high, low = split(total_y)
    wait(7, 11)
    turned = dot(high, swap[...]) + dot(low, swap[...])
    fill = jnp.zeros((ND - BX, ND), f32)
    total_y = jnp.concatenate([total_y, fill], axis=0).T
    turned = jnp.concatenate([turned, fill], axis=0).T
    lines_x = blockwise(total_x.T, y_inverse)
    lines_y = per_column(total_y, turned, x_inverse[...])
    both = times_left(grid_back[...], jnp.concatenate([lines_x, lines_y], axis=1))
    own_x, own_y = both[:, :BY], both[:, BY:]
    next_x = pltpu.roll(own_x, ND - RY, axis=0)
    next_y = pltpu.roll(own_y.reshape(CX, RY, BY), RY - 1, axis=1).reshape(ND, BY)
    answer[pl.ds(0, ND, stride=4), :] = own_x
    answer[pl.ds(1, ND, stride=4), :] = next_x
    answer[pl.ds(2, ND, stride=4), :] = own_y + pltpu.roll(next_y, BX, axis=1)
    answer[pl.ds(3, ND, stride=4), :] = jnp.zeros((ND, BY), f32)
    answer_copy = pltpu.make_async_copy(answer, answer_hbm, last_sem.at[0])
    answer_copy.start()
    answer_copy.wait()


def skeleton_solve(received, mode_eigen, tables):
    held = [received] + [tables[name] for name in skeleton_names]
    return pl.pallas_call(
        skeleton_kernel,
        in_specs=[pl.BlockSpec(memory_space=pltpu.SMEM)] + [any_spec] * 11,
        out_specs=any_spec,
        out_shape=jax.ShapeDtypeStruct((4 * ND, BY), f32),
        scratch_shapes=shapes_of(held)
        + [
            pltpu.VMEM((4 * ND, BY), f32),
            pltpu.SemaphoreType.DMA((11,)),
            pltpu.SemaphoreType.DMA((1,)),
        ],
        compiler_params=pltpu.CompilerParams(vmem_limit_bytes=GRANT),
    )(mode_eigen, *held)


correct_names = (
    "factors",
    "plain_sines",
    "near_far",
    "vertical",
    "vertical_right",
    "from_waves",
)


def correct_kernel(*refs):
    before_hbm, inputs = refs[0], refs[1:10]
    new_hbm, pressure_hbm, held, refs = refs[11], refs[12], refs[13:22], refs[22:]
    answer, waves, factors, plain_sines, near_far = held[:5]
    vertical, vertical_right, from_waves, heights = held[5:]
    velocity, pressure, reduced, in_sem, out_sem, pressure_sem, held_sem = refs
    copies = fetches(inputs, held, held_sem)

    def pressure_copy(part):
        levels = pl.ds(part * CHUNK, CHUNK)
        return pltpu.make_async_copy(
            pressure.at[levels, pl.ds(0, BX)], pressure_hbm.at[levels], pressure_sem.at[part]
        )

    def out_copy(part):
        levels = pl.ds(part * CHUNK, CHUNK)
        return pltpu.make_async_copy(
            velocity.at[:, levels], new_hbm.at[pl.ds(0, 3), levels], out_sem.at[part]
        )

    for copy in copies[:5]:
        copy.wait()
    for part in range(PARTS):
        part_copy(before_hbm, velocity, in_sem, part).start()
    own_x = answer[pl.ds(0, NZ, stride=4), :]
    next_x = answer[pl.ds(1, NZ, stride=4), :]
    lines_y = answer[pl.ds(2, NZ, stride=4), :]
    lane_z = lane_index(NZ)
    near, far = near_far[0:1], near_far[1:2]
    for i in range(1, BX):
        rhs = waves[i - 1] + lines_y[:, i : i + 1] * near + lines_y[:, BX + i : BX + i + 1] * far
        if i == 1:
            rhs = rhs + times_right(own_x, plain_sines[...])
        if i == BX - 1:
            rhs = rhs + times_right(next_x, plain_sines[...])
        reduced[i - 1] = rhs
    eliminate(reduced, factors, reduced)

    for copy in copies[5:]:
        copy.wait()
    rows = pressure.reshape(NZ * TALL, BY)
    rows[pl.ds(0, NZ, stride=TALL), :] = times_left(vertical[...], own_x)
    rows[pl.ds(BX, NZ, stride=TALL), :] = times_left(vertical[...], next_x)
    for i in range(1, BX):
        merged = jnp.where(lane_z == 0, lines_y[:, i : i + 1], reduced[i - 1])
        along_y = times_right(merged, from_waves[...])
        rows[pl.ds(i, NZ, stride=TALL), :] = times_left(vertical[...], along_y)
    tall = jnp.concatenate([lines_y, jnp.zeros((BY - NZ, BY), f32)], axis=0).T
    north = times_right(tall[BX : 2 * BX, :NZ], vertical_right[...])
    north = jnp.concatenate([north, jnp.zeros((BX, BY - NZ), f32)], axis=1)

    lane = lane_index(BX)

    def part_step(part, here):
        part_copy(before_hbm, velocity, in_sem, part).wait()
        sides = aligned(north, part, BY - 1)
        for sub in range(CHUNK):
            level = part * CHUNK + sub
            _, above_level = near_levels(level, sub)
            above = pressure[above_level, 0:BX]
            if sub == CHUNK - 1:
                above = jnp.where(level == NZ - 1, -here, above)
            east = pressure[level, 1 : BX + 1]
            side = jnp.where(
                lane == BY - 1, turned_back(sides, sub), pltpu.roll(here, BY - 1, axis=1)
            )
            factor = jnp.where(level >= heights[...], 0.25, 0.0).astype(f32)
            velocity[0, level] = velocity[0, level] - factor * (east - here)
            velocity[1, level] = velocity[1, level] - factor * (side - here)
            velocity[2, level] = velocity[2, level] - factor * (above - here)
            here = above
        out_copy(part).start()
        pressure_copy(part).start()
        return here

    lax.fori_loop(0, PARTS, part_step, pressure[0, 0:BX])
    for part in range(PARTS):
        out_copy(part).wait()
        pressure_copy(part).wait()


def corrected(before, waves, answer, heights, scalars, tables):
    held = [answer, waves] + [tables[name] for name in correct_names] + [heights]
    return pl.pallas_call(
        correct_kernel,
        in_specs=[any_spec] * 11,
        out_specs=[any_spec, any_spec],
        out_shape=[
            jax.ShapeDtypeStruct((5, NZ, BX, BY), f32),
            jax.ShapeDtypeStruct((NZ, BX, BY), f32),
        ],
        scratch_shapes=shapes_of(held)
        + [
            pltpu.VMEM((3, NZ, BX, BY), f32),
            pltpu.VMEM((NZ, TALL, BY), f32),
            pltpu.VMEM((BX - 1, NZ, BY), f32),
            pltpu.SemaphoreType.DMA((PARTS,)),
            pltpu.SemaphoreType.DMA((PARTS,)),
            pltpu.SemaphoreType.DMA((PARTS,)),
            pltpu.SemaphoreType.DMA((9,)),
        ],
        input_output_aliases={10: 0},
        compiler_params=pltpu.CompilerParams(vmem_limit_bytes=GRANT),
    )(before, *held, scalars)


def ring(value, axis, step):
    count = lax.axis_size(axis)
    return lax.ppermute(value, axis, [(n, (n + step) % count) for n in range(count)])


def exchanged(value):
    value = value.reshape(ND, 4, BY)
    return lax.all_to_all(value, ("col", "row"), 0, 0, tiled=True).reshape(4 * ND, BY)


def on_device(fields, heights, wall_class):
    block = {name: jnp.asarray(table) for name, table in block_tables().items()}
    skeleton = {name: jnp.asarray(table) for name, table in skeleton_tables().items()}
    first_x, last_x, first_y, last_y = block_edges(fields)
    west = ring(last_x, "col", 1)
    east = ring(first_x, "col", -1)
    south = ring(last_y, "row", 1)
    north = ring(first_y, "row", -1)
    before, waves, condensed = condensed_source(
        fields, wall_class, heights, west, east, south, north, block
    )
    received = exchanged(condensed)
    scalars = new_scalars(fields, wall_class, heights, west, east, south, north)
    mode = lax.axis_index("col") * RY + lax.axis_index("row")
    eigen = 2.0 - 2.0 * np.cos(np.pi * (np.arange(ND) + 0.5) / NZ)
    eigen[NZ:] = 1.0
    mode_eigen = lax.dynamic_slice(jnp.asarray(eigen.astype(np.float32)), (mode,), (1,))
    solved = skeleton_solve(received, mode_eigen, skeleton)
    answer = exchanged(solved)
    return tuple(corrected(before, waves, answer, heights, scalars, block))


def solution(mesh):
    in_specs = (P(None, None, "col", "row"), P("col", "row"), P(None, "col", "row"))
    out_specs = (P(None, None, "col", "row"), P(None, "col", "row"))
    return jax.shard_map(
        on_device, mesh=mesh, in_specs=in_specs, out_specs=out_specs, check_vma=False
    )
```

time: 117 us -> 88.6 us (0.76)
  Pallas kernels: 62.6 us -> 44.3 us
  blocking collectives: 15.3 us -> 0 us
  starting transfers between devices: 17.5 us -> 23.5 us
  local copies, waits for them, and re-layouts: 6.24 us -> 1.24 us
  waiting for transfers between devices: 14.7 us -> 18.4 us
    pallas_call x3 -> x4, Pallas kernels: 57.2 us -> 39 us  [the longest x1 17 us: condensed_source(): pl.pallas_call(source_kernel, in_specs=[any_spec] * 13, out_specs=[any_sp...]
    all_to_all x1 -> x0, blocking collectives: 15.3 us -> none  [on_device(): answer = lax.all_to_all(solved, ('col', 'row'), 0, 0, tiled=True)]
    all_to_all x1 -> x2, starting transfers between devices: 8.38 us -> 14.3 us  [exchanged(): lax.all_to_all(value, ('col', 'row'), 0, 0, tiled=True).reshape(4 * ND, BY)]
    all_to_all x4 -> x0, local copies, waits for them, and re-layouts: 4.25 us -> none  [the longest x2 2.48 us: on_device(): received = lax.all_to_all(condensed, ('col', 'row'), 0, 0, tiled=True)]
    all_to_all x1 -> x2, waiting for transfers between devices: 10.3 us -> 13.3 us  [exchanged(): lax.all_to_all(value, ('col', 'row'), 0, 0, tiled=True).reshape(4 * ND, BY)]
    unnamed x10 -> x0, local copies, waits for them, and re-layouts: 1.4 us -> none
  transfers between devices with their start and end apart: 5 -> 6, of which waited for: 3 -> 4; matrix products, arithmetic and copies ran while one was open for 1% -> 1% of each run, Pallas kernels for 0% -> 8%
where the time goes in v2:
time: 88.6 us; the launch traced here: 88.2 us
  Pallas kernels  44.3 us (50%)
  starting transfers between devices  23.5 us (27%)
  waiting for transfers between devices  18.4 us (21%)
  local copies, waits for them, and re-layouts  1.24 us (1%)
    pallas_call x1, Pallas kernels, condensed_source(): pl.pallas_call(source_kernel, in_specs=[any_spec] * 13, out_specs=[any_sp...  17 us
    all_to_all x2, starting transfers between devices, exchanged(): lax.all_to_all(value, ('col', 'row'), 0, 0, tiled=True).reshape(4 * ND, BY)  14.3 us
    all_to_all x2, waiting for transfers between devices, exchanged(): lax.all_to_all(value, ('col', 'row'), 0, 0, tiled=True).reshape(4 * ND, BY)  13.3 us
    pallas_call x1, Pallas kernels, corrected(): pl.pallas_call(correct_kernel, in_specs=[any_spec] * 11, out_specs=[any_s...  10 us
    ppermute x4, starting transfers between devices, ring(): lax.ppermute(value, axis, [(n, (n + step) % count) for n in range(count)])  9.24 us
    pallas_call x1, Pallas kernels, new_scalars(): pl.pallas_call(scalar_kernel, in_specs=[any_spec] * 7, out_specs=any_spec...  6.72 us
    pallas_call x1, Pallas kernels, skeleton_solve(): pl.pallas_call(skeleton_kernel, in_specs=[pl.BlockSpec(memory_space=pltpu...  5.27 us
    pallas_call x1, Pallas kernels, block_edges(): pl.pallas_call(edge_kernel, in_specs=[any_spec], out_specs=[any_spec] * 4...  5.23 us
  transfers between devices with their start and end apart: 6, of which 4 were waited for; matrix products, arithmetic and copies ran while one was open for 1% of the time, Pallas kernels for 8%

profile of v2, /device:TPU:1, one launch (start us, length us, event | category | flops | bytes accessed | tf_op | source)
XLA Modules:
  0.0 88.2 jit_solution(1263848677534758824)
XLA Ops:
  0.6 5.2 %shard_map.230 = (f32[480,128]{1,0:T(8,128)}, f32[480,128]{1,0:T(8,128)}, f32[10,32,128]{2,1,0:T(8,128)}, f32[10,32,128]{2,1,0:T(8,128)}) custom-call(f32[5,96,32,128]{3,2,1,0:T(8,128)} %refs_0_.3), custom_call_target="tpu_custom_call" | custom-call | tf_op jit(solution)/shard_map/pallas_call | solution.py:205
  5.9 2.5 %collective-permute-start = (f32[480,128]{1,0:T(8,128)}, f32[480,128]{1,0:T(8,128)}, u32[]{:S(2)}, u32[]{:S(2)}) collective-permute-start(f32[480,128]{1,0:T(8,128)} %get-tuple-element.9), channel_id=1, source_target_pairs={{0,1},{1,2},{2,3},{3,4},{4,5},{5,6},{6,7},{7,8},{8,9},{9,10},{10,1... | collective-permute-start | bytes 737288 | tf_op jit(solution)/shard_map/ppermute | solution.py:804
  8.4 4.7 %collective-permute-start.1 = (f32[480,128]{1,0:T(8,128)}, f32[480,128]{1,0:T(8,128)}, u32[]{:S(2)}, u32[]{:S(2)}) collective-permute-start(f32[480,128]{1,0:T(8,128)} %get-tuple-element.10), channel_id=1, source_target_pairs={{0,15},{1,0},{2,1},{3,2},{4,3},{5,4},{6,5},{7,6},{8,7},{9,8},{10,9... | collective-permute-start | bytes 737288 | tf_op jit(solution)/shard_map/ppermute | solution.py:804
  13.1 2.1 %collective-permute-start.2 = (f32[10,32,128]{2,1,0:T(8,128)}, f32[10,32,128]{2,1,0:T(8,128)}, u32[]{:S(2)}, u32[]{:S(2)}) collective-permute-start(f32[10,32,128]{2,1,0:T(8,128)} %get-tuple-element.11), channel_id=1, source_target_pairs={{0,16},{16,32},{32,48},{48,64},{64,80},{80,96},{96,112},{112,0},{1... | collective-permute-start | bytes 491528 | tf_op jit(solution)/shard_map/ppermute | solution.py:804
  15.1 0.0 collective-permute-start.3
  15.1 2.6 %collective-permute-done.2.refs_5_ = f32[10,32,128]{2,1,0:T(8,128)} collective-permute-done((f32[10,32,128]{2,1,0:T(8,128)}, f32[10,32,128]{2,1,0:T(8,128)}, u32[]{:S(2)}, u32[]{:S(2)}) %collective-permute-start.2) | collective-permute-done | bytes 163872 | tf_op jit(solution)/shard_map/ppermute | solution.py:804
  17.7 2.5 %collective-permute-done.3.refs_6_ = f32[10,32,128]{2,1,0:T(8,128)} collective-permute-done((f32[10,32,128]{2,1,0:T(8,128)}, f32[10,32,128]{2,1,0:T(8,128)}, u32[]{:S(2)}, u32[]{:S(2)}) %collective-permute-start.3) | collective-permute-done | bytes 163872 | tf_op jit(solution)/shard_map/ppermute | solution.py:804
  20.2 0.0 collective-permute-done.refs_3_
  20.2 0.0 collective-permute-done.1.refs_4_
  20.2 17.0 %shard_map.231 = (f32[3,96,32,128]{3,2,1,0:T(8,128)}, f32[31,96,128]{2,1,0:T(8,128)}, f32[512,128]{1,0:T(8,128)}) custom-call(f32[5,96,32,128]{3,2,1,0:T(8,128)} %refs_0_.3, s32[96,32,128]{2,1,0:T(8,128)} %refs_1_.4, s32[32,128]{1,0:T(8,128)} %refs_9_.3, f32[480,128]{1,0:T(8,128)} %collective-permute-done.refs_3_, ...), custom_call_target="tpu_custom_call" | custom-call | bytes 40000000 | tf_op jit(solution)/shard_map/pallas_call | solution.py:443
  37.2 9.0 %all-to-all-start = ((f32[128,4,128]{2,1,0:T(4,128)}), f32[128,4,128]{2,1,0:T(4,128)}, u32[]{:S(2)}, u32[]{:S(2)}) async-start(f32[128,4,128]{2,1,0:T(4,128)} %bitcast.5), calls=%async_computation | async-start | bytes 524288 | tf_op jit(solution)/shard_map/all_to_all | solution.py:809
  46.1 1.2 %dynamic_slice.3.mode_eigen = f32[1]{0:T(128)} dynamic-slice(f32[128]{0:T(128)} %constant.74.clone, s32[]{:T(128)S(6)} %select_n.3), dynamic_slice_sizes={1} | dynamic-slice | bytes 12 | tf_op jit(solution)/shard_map/dynamic_slice | solution.py:828
  47.4 9.3 %all-to-all-done = f32[128,4,128]{2,1,0:T(4,128)} async-done(((f32[128,4,128]{2,1,0:T(4,128)}), f32[128,4,128]{2,1,0:T(4,128)}, u32[]{:S(2)}, u32[]{:S(2)}) %all-to-all-start) | async-done | bytes 262176 | tf_op jit(solution)/shard_map/all_to_all | solution.py:809
  56.7 5.3 %shard_map.232 = f32[512,128]{1,0:T(8,128)} custom-call(f32[1]{0:T(128)} %dynamic_slice.3.mode_eigen, f32[512,128]{1,0:T(8,128)} %bitcast.1.refs_0_, bf16[256,256]{1,0:T(8,128)(2,1)} %constant.64.clone.refs_1_, bf16[256,256]{1,0:T(8,128)(2,1)} %constant.65.clone.refs_2_, bf16[8,256,256]{2,1,0:T(8,128)(2,1)} %constant.67.clone.refs_3_, ...), custom_call_target="tpu_custom_call" | custom-call | tf_op jit(solution)/shard_map/pallas_call | solution.py:671
  62.0 5.3 %all-to-all-start.1 = ((f32[128,4,128]{2,1,0:T(4,128)}), f32[128,4,128]{2,1,0:T(4,128)}, u32[]{:S(2)}, u32[]{:S(2)}) async-start(f32[128,4,128]{2,1,0:T(4,128)} %bitcast.4), calls=%async_computation.1 | async-start | bytes 524288 | tf_op jit(solution)/shard_map/all_to_all | solution.py:809
  67.3 6.7 %shard_map.233.refs_10_ = f32[5,96,32,128]{3,2,1,0:T(8,128)} custom-call(f32[5,96,32,128]{3,2,1,0:T(8,128)} %refs_0_.3, s32[96,32,128]{2,1,0:T(8,128)} %refs_1_.4, s32[32,128]{1,0:T(8,128)} %refs_9_.3, f32[480,128]{1,0:T(8,128)} %collective-permute-done.refs_3_, f32[480,128]{1,0:T(8,128)} %collective-permute-done.1.refs_4_, ...), custom_call_target="tpu_custom_call" | custom-call | bytes 30000000 | tf_op jit(solution)/shard_map/pallas_call | solution.py:550
  74.0 4.0 %all-to-all-done.1 = f32[128,4,128]{2,1,0:T(4,128)} async-done(((f32[128,4,128]{2,1,0:T(4,128)}), f32[128,4,128]{2,1,0:T(4,128)}, u32[]{:S(2)}, u32[]{:S(2)}) %all-to-all-start.1) | async-done | bytes 262176 | tf_op jit(solution)/shard_map/all_to_all | solution.py:809
  78.0 10.0 %shard_map.234 = (f32[5,96,32,128]{3,2,1,0:T(8,128)}, f32[96,32,128]{2,1,0:T(8,128)}) custom-call(f32[3,96,32,128]{3,2,1,0:T(8,128)} %get-tuple-element.13.refs_0_, f32[512,128]{1,0:T(8,128)} %bitcast.3.refs_1_, f32[31,96,128]{2,1,0:T(8,128)} %get-tuple-element.15.refs_2_, ...), custom_call_target="tpu_custom_call", output_to_operand_aliasing={{0}: (10, {})} | custom-call | tf_op jit(solution)/shard_map/pallas_call | solution.py:779
Async XLA Ops:
  5.9 14.3 %collective-permute-start = (f32[480,128]{1,0:T(8,128)}, f32[480,128]{1,0:T(8,128)}, u32[]{:S(2)}, u32[]{:S(2)}) collective-permute-start(f32[480,128]{1,0:T(8,128)} %get-tuple-element.9), channel_id=1, source_target_pairs={{0,1},{1,2},{2,3},{3,4},{4,5},{5,6},{6,7},{7,8},{8,9},{9,10},{10,1... | collective-permute-start | bytes 737288 | tf_op jit(solution)/shard_map/ppermute | solution.py:804
  8.4 11.8 %collective-permute-start.1 = (f32[480,128]{1,0:T(8,128)}, f32[480,128]{1,0:T(8,128)}, u32[]{:S(2)}, u32[]{:S(2)}) collective-permute-start(f32[480,128]{1,0:T(8,128)} %get-tuple-element.10), channel_id=1, source_target_pairs={{0,15},{1,0},{2,1},{3,2},{4,3},{5,4},{6,5},{7,6},{8,7},{9,8},{10,9... | collective-permute-start | bytes 737288 | tf_op jit(solution)/shard_map/ppermute | solution.py:804
  13.1 4.6 %collective-permute-start.2 = (f32[10,32,128]{2,1,0:T(8,128)}, f32[10,32,128]{2,1,0:T(8,128)}, u32[]{:S(2)}, u32[]{:S(2)}) collective-permute-start(f32[10,32,128]{2,1,0:T(8,128)} %get-tuple-element.11), channel_id=1, source_target_pairs={{0,16},{16,32},{32,48},{48,64},{64,80},{80,96},{96,112},{112,0},{1... | collective-permute-start | bytes 491528 | tf_op jit(solution)/shard_map/ppermute | solution.py:804
  15.1 5.1 %collective-permute-start.3 = (f32[10,32,128]{2,1,0:T(8,128)}, f32[10,32,128]{2,1,0:T(8,128)}, u32[]{:S(2)}, u32[]{:S(2)}) collective-permute-start(f32[10,32,128]{2,1,0:T(8,128)} %get-tuple-element.12), channel_id=1, source_target_pairs={{0,112},{16,0},{32,16},{48,32},{64,48},{80,64},{96,80},{112,96},{1... | collective-permute-start | bytes 491528 | tf_op jit(solution)/shard_map/ppermute | solution.py:804
  37.2 19.5 %all-to-all-start = ((f32[128,4,128]{2,1,0:T(4,128)}), f32[128,4,128]{2,1,0:T(4,128)}, u32[]{:S(2)}, u32[]{:S(2)}) async-start(f32[128,4,128]{2,1,0:T(4,128)} %bitcast.5), calls=%async_computation | async-start | bytes 524288 | tf_op jit(solution)/shard_map/all_to_all | solution.py:809
  62.0 16.0 %all-to-all-start.1 = ((f32[128,4,128]{2,1,0:T(4,128)}), f32[128,4,128]{2,1,0:T(4,128)}, u32[]{:S(2)}, u32[]{:S(2)}) async-start(f32[128,4,128]{2,1,0:T(4,128)} %bitcast.4), calls=%async_computation.1 | async-start | bytes 524288 | tf_op jit(solution)/shard_map/all_to_all | solution.py:809

commit v3 on v2

--- a/solution.py
+++ b/solution.py
@@ -74,7 +74,7 @@
     return dict(
         vertical=left_stack(vertical),
         vertical_right=right_stack(vertical),
-        to_waves=right_stack(to_waves),
+        to_waves=right_stack(-4.0 * to_waves),
         plain_sines=right_stack(sines),
         edge_rows=right_stack(edge_rows),
         from_waves=right_stack(from_waves),
@@ -323,11 +323,11 @@
     inputs, refs = refs[2:13], refs[13:]
     new_hbm, waves_hbm, condensed_hbm = refs[:3]
     held, refs = refs[3:14], refs[14:]
-    heights, west, east, south, north = held[:5]
-    vertical, vertical_right, to_waves, edge_rows, edges, factors = held[5:]
-    fields, wall, new, source, waves, reduced, condensed, sides = refs[:8]
-    in_sem, wall_sem, out_sem, held_sem, last_sem = refs[8:]
-    copies = fetches(inputs[:5], held[:5], held_sem)
+    heights, west, east, south, north, to_waves = held[:6]
+    vertical, vertical_right, edge_rows, edges, factors = held[6:]
+    fields, wall, new, source, waves, reduced, condensed, sides, ends_x = refs[:9]
+    in_sem, wall_sem, out_sem, held_sem, last_sem = refs[9:]
+    copies = fetches(inputs[:6], held[:6], held_sem)
 
     def field_copy(part):
         levels = pl.ds(part * CHUNK, CHUNK)
@@ -340,7 +340,7 @@
     for part in range(PARTS):
         field_copy(part).start()
         part_copy(wall_hbm, wall, wall_sem, part).start()
-    tables = fetches(inputs[5:], held[5:], held_sem.at[pl.ds(5, 6)])
+    tables = fetches(inputs[6:], held[6:], held_sem.at[pl.ds(6, 5)])
     for copy in copies:
         copy.wait()
     put_rows(fields, west, east, range(3))
@@ -351,15 +351,38 @@
     row = row_index(BX)
     zero = jnp.zeros((BX, BY), f32)
 
-    def part_step(part, carry):
+    def spread(part):
+        pieces = []
+        ends = zero
+        for sub in range(CHUNK):
+            level = part * CHUNK + sub
+            u, v, w = new[0, level], new[1, level], new[2, level]
+            if sub:
+                w_below = new[2, level - 1]
+            else:
+                w_below = jnp.where(part > 0, new[2, jnp.maximum(level - 1, 0)], 0.0)
+            u_behind = jnp.where(row == 0, 0.0, pltpu.roll(u, 1, axis=0))
+            v_behind = pltpu.roll(v, 1, axis=1)
+            ends = jnp.where(lane == sub, turned_back(v_behind, BY - sub), ends)
+            v_behind = jnp.where(lane == 0, 0.0, v_behind)
+            divergence = (u - u_behind) + (v - v_behind) + (w - w_below)
+            ends_x[pl.ds(level, 1), :] = -4.0 * divergence[:1]
+            ends_x[pl.ds(NZ + level, 1), :] = 4.0 * u[BX - 1 :]
+            pieces.append(divergence)
+        along_y = times_right(jnp.concatenate(pieces, axis=0), to_waves[...])
+        for sub in range(CHUNK):
+            rows = pl.ds(part * CHUNK + sub, BX, stride=NZ)
+            source[rows, :] = along_y[sub * BX : (sub + 1) * BX]
+        return pltpu.roll(ends, part * CHUNK, axis=1)
+
+    def part_step(part, v_edge):
         @pl.when(part < PARTS - 1)
         def _():
             field_copy(part + 1).wait()
 
         part_copy(wall_hbm, wall, wall_sem, part).wait()
-        w_below, v_edge = carry
+        v_edge = v_edge + jnp.where(part > 0, spread(jnp.maximum(part - 1, 0)), 0.0)
         turned = [part_sides(sides, n, part) for n in range(3)]
-        ends = zero
         for sub in range(CHUNK):
             level = part * CHUNK + sub
             below, above = near_levels(level, sub)
@@ -368,9 +391,8 @@
             coefs = coefficients(u, v, w, fluid)
             speed = jnp.sqrt(u * u + v * v + w * w + 0.01)
             own = fluid * (0.85 - 0.2 * wall[level].astype(f32) * speed)
-            results = []
             for n, f in enumerate((u, v, w)):
-                total = own * f + neighbour_sum(
+                new[n, level] = own * f + neighbour_sum(
                     fields,
                     n,
                     level,
@@ -382,30 +404,23 @@
                     coefs,
                     lane,
                 )
-                new[n, level] = total
-                results.append(total)
-            u_new, v_new, w_new = results
-            u_behind = jnp.where(row == 0, 0.0, pltpu.roll(u_new, 1, axis=0))
-            v_behind = pltpu.roll(v_new, 1, axis=1)
-            ends = jnp.where(lane == sub, turned_back(v_behind, BY - sub), ends)
-            v_behind = jnp.where(lane == 0, 0.0, v_behind)
-            divergence = (u_new - u_behind) + (v_new - v_behind) + (w_new - w_below)
-            source[pl.ds(level, BX, stride=NZ), :] = -4.0 * divergence
-            source[pl.ds(BX * NZ + level, 1), :] = 4.0 * u_new[BX - 1 :]
-            w_below = w_new
-        v_edge = v_edge + pltpu.roll(ends, part * CHUNK, axis=1)
         part_copy(new, new_hbm, out_sem, part).start()
-        return w_below, v_edge
-
-    _, v_edge = lax.fori_loop(0, PARTS, part_step, (zero, zero))
-
+        return v_edge
+
+    v_edge = lax.fori_loop(0, PARTS, part_step, zero)
+
+    v_edge = v_edge + spread(PARTS - 1)
     for copy in tables:
         copy.wait()
-    for i in range(1, BX):
-        along_y = times_right(source[i * NZ : (i + 1) * NZ, :], to_waves[...])
-        waves[i - 1] = times_left(vertical[...], along_y)
-    own_x = times_left(vertical[...], source[0:NZ, :])
-    next_x = times_left(vertical[...], source[BX * NZ : (BX + 1) * NZ, :])
+    for i in range(1, BX - 1, 2):
+        pair = [source[n * NZ : (n + 1) * NZ, :] for n in (i, i + 1)]
+        out = times_left(vertical[...], jnp.concatenate(pair, axis=1))
+        waves[i - 1] = out[:, :BY]
+        waves[i] = out[:, BY:]
+    waves[BX - 2] = times_left(vertical[...], source[(BX - 1) * NZ : BX * NZ, :])
+    pair = jnp.concatenate([ends_x[0:NZ, :], ends_x[NZ : 2 * NZ, :]], axis=1)
+    out = times_left(vertical[...], pair)
+    own_x, next_x = out[:, :BY], out[:, BY:]
 
     waves_copy = pltpu.make_async_copy(waves, waves_hbm, last_sem.at[0])
     waves_copy.start()
@@ -438,7 +453,7 @@
 
 
 def condensed_source(fields, wall_class, heights, west, east, south, north, tables):
-    names = ("vertical", "vertical_right", "to_waves", "edge_rows", "edges", "factors")
+    names = ("to_waves", "vertical", "vertical_right", "edge_rows", "edges", "factors")
     held = [heights, west, east, south, north] + [tables[name] for name in names]
     return pl.pallas_call(
         source_kernel,
@@ -454,11 +469,12 @@
             pltpu.VMEM((3, NZ, ROWS, BY), f32),
             pltpu.VMEM((NZ, BX, BY), jnp.int32),
             pltpu.VMEM((3, NZ, BX, BY), f32),
-            pltpu.VMEM(((BX + 1) * NZ, BY), f32),
+            pltpu.VMEM((BX * NZ, BY), f32),
             pltpu.VMEM((BX - 1, NZ, BY), f32),
             pltpu.VMEM((BX - 1, NZ, BY), f32),
             pltpu.VMEM((4 * ND, BY), f32),
             pltpu.VMEM((10, BX, BY), f32),
+            pltpu.VMEM((2 * NZ, BY), f32),
             pltpu.SemaphoreType.DMA((PARTS,)),
             pltpu.SemaphoreType.DMA((PARTS,)),
             pltpu.SemaphoreType.DMA((PARTS,)),
@@ -698,8 +714,15 @@
     new_hbm, pressure_hbm, held, refs = refs[11], refs[12], refs[13:22], refs[22:]
     answer, waves, factors, plain_sines, near_far = held[:5]
     vertical, vertical_right, from_waves, heights = held[5:]
-    velocity, pressure, reduced, in_sem, out_sem, pressure_sem, held_sem = refs
-    copies = fetches(inputs, held, held_sem)
+    velocity, pressure, reduced, in_sem, out_sem, pressure_sem, held_sem, row_sem = refs
+    first = [pl.ds(0, 8), pl.ds(8, 8), pl.ds(16, BX - 17)]
+    copies = fetches(inputs[:1], held[:1], held_sem)
+    rows_in = []
+    for number, rows in enumerate(first):
+        pair = [inputs[1].at[rows], inputs[2].at[rows]]
+        held_pair = [waves.at[rows], factors.at[rows]]
+        rows_in.append(fetches(pair, held_pair, row_sem.at[pl.ds(2 * number, 2)]))
+    copies += fetches(inputs[3:], held[3:], held_sem.at[pl.ds(1, 6)])
 
     def pressure_copy(part):
         levels = pl.ds(part * CHUNK, CHUNK)
@@ -713,7 +736,7 @@
             velocity.at[:, levels], new_hbm.at[pl.ds(0, 3), levels], out_sem.at[part]
         )
 
-    for copy in copies[:5]:
+    for copy in copies[:3]:
         copy.wait()
     for part in range(PARTS):
         part_copy(before_hbm, velocity, in_sem, part).start()
@@ -723,6 +746,9 @@
     lane_z = lane_index(NZ)
     near, far = near_far[0:1], near_far[1:2]
     for i in range(1, BX):
+        if i in (1, 9, 17):
+            for copy in rows_in[i // 8]:
+                copy.wait()
         rhs = waves[i - 1] + lines_y[:, i : i + 1] * near + lines_y[:, BX + i : BX + i + 1] * far
         if i == 1:
             rhs = rhs + times_right(own_x, plain_sines[...])
@@ -731,15 +757,19 @@
         reduced[i - 1] = rhs
     eliminate(reduced, factors, reduced)
 
-    for copy in copies[5:]:
+    for copy in copies[3:]:
         copy.wait()
     rows = pressure.reshape(NZ * TALL, BY)
-    rows[pl.ds(0, NZ, stride=TALL), :] = times_left(vertical[...], own_x)
-    rows[pl.ds(BX, NZ, stride=TALL), :] = times_left(vertical[...], next_x)
+    planes = [own_x]
     for i in range(1, BX):
         merged = jnp.where(lane_z == 0, lines_y[:, i : i + 1], reduced[i - 1])
-        along_y = times_right(merged, from_waves[...])
-        rows[pl.ds(i, NZ, stride=TALL), :] = times_left(vertical[...], along_y)
+        planes.append(times_right(merged, from_waves[...]))
+        if i % 2:
+            out = times_left(vertical[...], jnp.concatenate(planes, axis=1))
+            rows[pl.ds(i - 1, NZ, stride=TALL), :] = out[:, :BY]
+            rows[pl.ds(i, NZ, stride=TALL), :] = out[:, BY:]
+            planes = []
+    rows[pl.ds(BX, NZ, stride=TALL), :] = times_left(vertical[...], next_x)
     tall = jnp.concatenate([lines_y, jnp.zeros((BY - NZ, BY), f32)], axis=0).T
     north = times_right(tall[BX : 2 * BX, :NZ], vertical_right[...])
     north = jnp.concatenate([north, jnp.zeros((BX, BY - NZ), f32)], axis=1)
@@ -792,7 +822,8 @@
             pltpu.SemaphoreType.DMA((PARTS,)),
             pltpu.SemaphoreType.DMA((PARTS,)),
             pltpu.SemaphoreType.DMA((PARTS,)),
-            pltpu.SemaphoreType.DMA((9,)),
+            pltpu.SemaphoreType.DMA((7,)),
+            pltpu.SemaphoreType.DMA((6,)),
         ],
         input_output_aliases={10: 0},
         compiler_params=pltpu.CompilerParams(vmem_limit_bytes=GRANT),

time: 88.6 us -> 83.4 us (0.941)
  Pallas kernels: 44.3 us -> 39.3 us
    pallas_call x1, Pallas kernels: 17 us -> 12.5 us  [condensed_source(): pl.pallas_call(source_kernel, in_specs=[any_spec] * 13, out_specs=[any_sp...]
where the time goes in v3:
time: 83.4 us; the launch traced here: 83 us
  Pallas kernels  39.3 us (47%)
  starting transfers between devices  23.5 us (28%)
  waiting for transfers between devices  18.3 us (22%)
  local copies, waits for them, and re-layouts  1.24 us (1%)
    all_to_all x2, starting transfers between devices, exchanged(): lax.all_to_all(value, ('col', 'row'), 0, 0, tiled=True).reshape(4 * ND, BY)  14.3 us
    all_to_all x2, waiting for transfers between devices, exchanged(): lax.all_to_all(value, ('col', 'row'), 0, 0, tiled=True).reshape(4 * ND, BY)  13.3 us
    pallas_call x1, Pallas kernels, condensed_source(): pl.pallas_call(source_kernel, in_specs=[any_spec] * 13, out_specs=[any_sp...  12.5 us
    pallas_call x1, Pallas kernels, corrected(): pl.pallas_call(correct_kernel, in_specs=[any_spec] * 11, out_specs=[any_s...  9.58 us
    ppermute x4, starting transfers between devices, ring(): lax.ppermute(value, axis, [(n, (n + step) % count) for n in range(count)])  9.24 us
    pallas_call x1, Pallas kernels, new_scalars(): pl.pallas_call(scalar_kernel, in_specs=[any_spec] * 7, out_specs=any_spec...  6.72 us
    pallas_call x1, Pallas kernels, skeleton_solve(): pl.pallas_call(skeleton_kernel, in_specs=[pl.BlockSpec(memory_space=pltpu...  5.26 us
    pallas_call x1, Pallas kernels, block_edges(): pl.pallas_call(edge_kernel, in_specs=[any_spec], out_specs=[any_spec] * 4...  5.23 us
  transfers between devices with their start and end apart: 6, of which 4 were waited for; matrix products, arithmetic and copies ran while one was open for 1% of the time, Pallas kernels for 8%

profile of v3, /device:TPU:1, one launch (start us, length us, event | category | flops | bytes accessed | tf_op | source)
XLA Modules:
  0.0 83.0 jit_solution(11119549988782980953)
XLA Ops:
  0.6 5.2 %shard_map.230 = (f32[480,128]{1,0:T(8,128)}, f32[480,128]{1,0:T(8,128)}, f32[10,32,128]{2,1,0:T(8,128)}, f32[10,32,128]{2,1,0:T(8,128)}) custom-call(f32[5,96,32,128]{3,2,1,0:T(8,128)} %refs_0_.3), custom_call_target="tpu_custom_call" | custom-call | tf_op jit(solution)/shard_map/pallas_call | solution.py:205
  5.9 2.5 %collective-permute-start = (f32[480,128]{1,0:T(8,128)}, f32[480,128]{1,0:T(8,128)}, u32[]{:S(2)}, u32[]{:S(2)}) collective-permute-start(f32[480,128]{1,0:T(8,128)} %get-tuple-element.9), channel_id=1, source_target_pairs={{0,1},{1,2},{2,3},{3,4},{4,5},{5,6},{6,7},{7,8},{8,9},{9,10},{10,1... | collective-permute-start | bytes 737288 | tf_op jit(solution)/shard_map/ppermute | solution.py:835
  8.4 4.7 %collective-permute-start.1 = (f32[480,128]{1,0:T(8,128)}, f32[480,128]{1,0:T(8,128)}, u32[]{:S(2)}, u32[]{:S(2)}) collective-permute-start(f32[480,128]{1,0:T(8,128)} %get-tuple-element.10), channel_id=1, source_target_pairs={{0,15},{1,0},{2,1},{3,2},{4,3},{5,4},{6,5},{7,6},{8,7},{9,8},{10,9... | collective-permute-start | bytes 737288 | tf_op jit(solution)/shard_map/ppermute | solution.py:835
  13.1 2.1 %collective-permute-start.2 = (f32[10,32,128]{2,1,0:T(8,128)}, f32[10,32,128]{2,1,0:T(8,128)}, u32[]{:S(2)}, u32[]{:S(2)}) collective-permute-start(f32[10,32,128]{2,1,0:T(8,128)} %get-tuple-element.11), channel_id=1, source_target_pairs={{0,16},{16,32},{32,48},{48,64},{64,80},{80,96},{96,112},{112,0},{1... | collective-permute-start | bytes 491528 | tf_op jit(solution)/shard_map/ppermute | solution.py:835
  15.1 0.0 collective-permute-start.3
  15.1 2.6 %collective-permute-done.2.refs_5_ = f32[10,32,128]{2,1,0:T(8,128)} collective-permute-done((f32[10,32,128]{2,1,0:T(8,128)}, f32[10,32,128]{2,1,0:T(8,128)}, u32[]{:S(2)}, u32[]{:S(2)}) %collective-permute-start.2) | collective-permute-done | bytes 163872 | tf_op jit(solution)/shard_map/ppermute | solution.py:835
  17.7 2.5 %collective-permute-done.3.refs_6_ = f32[10,32,128]{2,1,0:T(8,128)} collective-permute-done((f32[10,32,128]{2,1,0:T(8,128)}, f32[10,32,128]{2,1,0:T(8,128)}, u32[]{:S(2)}, u32[]{:S(2)}) %collective-permute-start.3) | collective-permute-done | bytes 163872 | tf_op jit(solution)/shard_map/ppermute | solution.py:835
  20.2 0.0 collective-permute-done.refs_3_
  20.2 0.0 collective-permute-done.1.refs_4_
  20.2 12.5 %shard_map.231 = (f32[3,96,32,128]{3,2,1,0:T(8,128)}, f32[31,96,128]{2,1,0:T(8,128)}, f32[512,128]{1,0:T(8,128)}) custom-call(f32[5,96,32,128]{3,2,1,0:T(8,128)} %refs_0_.3, s32[96,32,128]{2,1,0:T(8,128)} %refs_1_.4, s32[32,128]{1,0:T(8,128)} %refs_9_.3, f32[480,128]{1,0:T(8,128)} %collective-permute-done.refs_3_, ...), custom_call_target="tpu_custom_call" | custom-call | bytes 40000000 | tf_op jit(solution)/shard_map/pallas_call | solution.py:458
  32.6 9.0 %all-to-all-start = ((f32[128,4,128]{2,1,0:T(4,128)}), f32[128,4,128]{2,1,0:T(4,128)}, u32[]{:S(2)}, u32[]{:S(2)}) async-start(f32[128,4,128]{2,1,0:T(4,128)} %bitcast.5), calls=%async_computation | async-start | bytes 524288 | tf_op jit(solution)/shard_map/all_to_all | solution.py:840
  41.6 1.2 %dynamic_slice.3.mode_eigen = f32[1]{0:T(128)} dynamic-slice(f32[128]{0:T(128)} %constant.74.clone, s32[]{:T(128)S(6)} %select_n.3), dynamic_slice_sizes={1} | dynamic-slice | bytes 12 | tf_op jit(solution)/shard_map/dynamic_slice | solution.py:859
  42.9 9.3 %all-to-all-done = f32[128,4,128]{2,1,0:T(4,128)} async-done(((f32[128,4,128]{2,1,0:T(4,128)}), f32[128,4,128]{2,1,0:T(4,128)}, u32[]{:S(2)}, u32[]{:S(2)}) %all-to-all-start) | async-done | bytes 262176 | tf_op jit(solution)/shard_map/all_to_all | solution.py:840
  52.2 5.3 %shard_map.232 = f32[512,128]{1,0:T(8,128)} custom-call(f32[1]{0:T(128)} %dynamic_slice.3.mode_eigen, f32[512,128]{1,0:T(8,128)} %bitcast.1.refs_0_, bf16[256,256]{1,0:T(8,128)(2,1)} %constant.64.clone.refs_1_, bf16[256,256]{1,0:T(8,128)(2,1)} %constant.65.clone.refs_2_, bf16[8,256,256]{2,1,0:T(8,128)(2,1)} %constant.67.clone.refs_3_, ...), custom_call_target="tpu_custom_call" | custom-call | tf_op jit(solution)/shard_map/pallas_call | solution.py:687
  57.4 5.3 %all-to-all-start.1 = ((f32[128,4,128]{2,1,0:T(4,128)}), f32[128,4,128]{2,1,0:T(4,128)}, u32[]{:S(2)}, u32[]{:S(2)}) async-start(f32[128,4,128]{2,1,0:T(4,128)} %bitcast.4), calls=%async_computation.1 | async-start | bytes 524288 | tf_op jit(solution)/shard_map/all_to_all | solution.py:840
  62.8 6.7 %shard_map.233.refs_10_ = f32[5,96,32,128]{3,2,1,0:T(8,128)} custom-call(f32[5,96,32,128]{3,2,1,0:T(8,128)} %refs_0_.3, s32[96,32,128]{2,1,0:T(8,128)} %refs_1_.4, s32[32,128]{1,0:T(8,128)} %refs_9_.3, f32[480,128]{1,0:T(8,128)} %collective-permute-done.refs_3_, f32[480,128]{1,0:T(8,128)} %collective-permute-done.1.refs_4_, ...), custom_call_target="tpu_custom_call" | custom-call | bytes 30000000 | tf_op jit(solution)/shard_map/pallas_call | solution.py:566
  69.5 4.0 %all-to-all-done.1 = f32[128,4,128]{2,1,0:T(4,128)} async-done(((f32[128,4,128]{2,1,0:T(4,128)}), f32[128,4,128]{2,1,0:T(4,128)}, u32[]{:S(2)}, u32[]{:S(2)}) %all-to-all-start.1) | async-done | bytes 262176 | tf_op jit(solution)/shard_map/all_to_all | solution.py:840
  73.5 9.6 %shard_map.234 = (f32[5,96,32,128]{3,2,1,0:T(8,128)}, f32[96,32,128]{2,1,0:T(8,128)}) custom-call(f32[3,96,32,128]{3,2,1,0:T(8,128)} %get-tuple-element.13.refs_0_, f32[512,128]{1,0:T(8,128)} %bitcast.3.refs_1_, f32[31,96,128]{2,1,0:T(8,128)} %get-tuple-element.15.refs_2_, ...), custom_call_target="tpu_custom_call", output_to_operand_aliasing={{0}: (10, {})} | custom-call | tf_op jit(solution)/shard_map/pallas_call | solution.py:809
Async XLA Ops:
  5.9 14.3 %collective-permute-start = (f32[480,128]{1,0:T(8,128)}, f32[480,128]{1,0:T(8,128)}, u32[]{:S(2)}, u32[]{:S(2)}) collective-permute-start(f32[480,128]{1,0:T(8,128)} %get-tuple-element.9), channel_id=1, source_target_pairs={{0,1},{1,2},{2,3},{3,4},{4,5},{5,6},{6,7},{7,8},{8,9},{9,10},{10,1... | collective-permute-start | bytes 737288 | tf_op jit(solution)/shard_map/ppermute | solution.py:835
  8.4 11.8 %collective-permute-start.1 = (f32[480,128]{1,0:T(8,128)}, f32[480,128]{1,0:T(8,128)}, u32[]{:S(2)}, u32[]{:S(2)}) collective-permute-start(f32[480,128]{1,0:T(8,128)} %get-tuple-element.10), channel_id=1, source_target_pairs={{0,15},{1,0},{2,1},{3,2},{4,3},{5,4},{6,5},{7,6},{8,7},{9,8},{10,9... | collective-permute-start | bytes 737288 | tf_op jit(solution)/shard_map/ppermute | solution.py:835
  13.1 4.6 %collective-permute-start.2 = (f32[10,32,128]{2,1,0:T(8,128)}, f32[10,32,128]{2,1,0:T(8,128)}, u32[]{:S(2)}, u32[]{:S(2)}) collective-permute-start(f32[10,32,128]{2,1,0:T(8,128)} %get-tuple-element.11), channel_id=1, source_target_pairs={{0,16},{16,32},{32,48},{48,64},{64,80},{80,96},{96,112},{112,0},{1... | collective-permute-start | bytes 491528 | tf_op jit(solution)/shard_map/ppermute | solution.py:835
  15.1 5.1 %collective-permute-start.3 = (f32[10,32,128]{2,1,0:T(8,128)}, f32[10,32,128]{2,1,0:T(8,128)}, u32[]{:S(2)}, u32[]{:S(2)}) collective-permute-start(f32[10,32,128]{2,1,0:T(8,128)} %get-tuple-element.12), channel_id=1, source_target_pairs={{0,112},{16,0},{32,16},{48,32},{64,48},{80,64},{96,80},{112,96},{1... | collective-permute-start | bytes 491528 | tf_op jit(solution)/shard_map/ppermute | solution.py:835
  32.6 19.5 %all-to-all-start = ((f32[128,4,128]{2,1,0:T(4,128)}), f32[128,4,128]{2,1,0:T(4,128)}, u32[]{:S(2)}, u32[]{:S(2)}) async-start(f32[128,4,128]{2,1,0:T(4,128)} %bitcast.5), calls=%async_computation | async-start | bytes 524288 | tf_op jit(solution)/shard_map/all_to_all | solution.py:840
  57.4 16.0 %all-to-all-start.1 = ((f32[128,4,128]{2,1,0:T(4,128)}), f32[128,4,128]{2,1,0:T(4,128)}, u32[]{:S(2)}, u32[]{:S(2)}) async-start(f32[128,4,128]{2,1,0:T(4,128)} %bitcast.4), calls=%async_computation.1 | async-start | bytes 524288 | tf_op jit(solution)/shard_map/all_to_all | solution.py:840

commit v4 on v3

--- a/solution.py
+++ b/solution.py
@@ -174,6 +174,20 @@
         copy(number).start()
     lane = lane_index(BX)
 
+    def out_copies(number):
+        plane = pl.ds(pl.multiple_of(number * NZ, NZ), NZ)
+        groups = pl.ds(2 * number, 2)
+        pairs = (
+            (east.at[plane], first_x.at[plane]),
+            (west.at[plane], last_x.at[plane]),
+            (north.at[groups], first_y.at[groups]),
+            (south.at[groups], last_y.at[groups]),
+        )
+        return [
+            pltpu.make_async_copy(source, target, out_sem.at[4 * number + index])
+            for index, (source, target) in enumerate(pairs)
+        ]
+
     def step(number, carry):
         copy(number).wait()
         rows = held.at[number].reshape(NZ * BX, BY)
@@ -189,13 +203,14 @@
                 last = jnp.where(lane == (2 * level - 1) % BY, turned, last)
             north[2 * number + group] = first
             south[2 * number + group] = last
+        for copied in out_copies(number):
+            copied.start()
         return carry
 
     lax.fori_loop(0, 5, step, 0)
-    for copied in fetches(
-        [east, west, north, south], [first_x, last_x, first_y, last_y], out_sem
-    ):
-        copied.wait()
+    for number in range(5):
+        for copied in out_copies(number):
+            copied.wait()
 
 
 def block_edges(fields):
@@ -209,7 +224,7 @@
         out_shape=[jax.ShapeDtypeStruct(shape, f32) for shape in shapes],
         scratch_shapes=[pltpu.VMEM((5, NZ, BX, BY), f32)]
         + [pltpu.VMEM(shape, f32) for shape in shapes]
-        + [pltpu.SemaphoreType.DMA((5,)), pltpu.SemaphoreType.DMA((4,))],
+        + [pltpu.SemaphoreType.DMA((5,)), pltpu.SemaphoreType.DMA((20,))],
         compiler_params=pltpu.CompilerParams(vmem_limit_bytes=GRANT),
     )(fields)
 

time: 83.4 us -> 83.1 us (level)
  transfers between devices with their start and end apart: 6 -> 6, of which waited for: 4 -> 4; matrix products, arithmetic and copies ran while one was open for 1% -> 2% of each run, Pallas kernels for 8% -> 8%
where the time goes in v4:
time: 83.1 us; the launch traced here: 82.7 us
  Pallas kernels  38.9 us (47%)
  starting transfers between devices  23.5 us (28%)
  waiting for transfers between devices  18.3 us (22%)
  local copies, waits for them, and re-layouts  1.24 us (1%)
    all_to_all x2, starting transfers between devices, exchanged(): lax.all_to_all(value, ('col', 'row'), 0, 0, tiled=True).reshape(4 * ND, BY)  14.3 us
    all_to_all x2, waiting for transfers between devices, exchanged(): lax.all_to_all(value, ('col', 'row'), 0, 0, tiled=True).reshape(4 * ND, BY)  13.3 us
    pallas_call x1, Pallas kernels, condensed_source(): pl.pallas_call(source_kernel, in_specs=[any_spec] * 13, out_specs=[any_sp...  12.5 us
    pallas_call x1, Pallas kernels, corrected(): pl.pallas_call(correct_kernel, in_specs=[any_spec] * 11, out_specs=[any_s...  9.58 us
    ppermute x4, starting transfers between devices, ring(): lax.ppermute(value, axis, [(n, (n + step) % count) for n in range(count)])  9.24 us
    pallas_call x1, Pallas kernels, new_scalars(): pl.pallas_call(scalar_kernel, in_specs=[any_spec] * 7, out_specs=any_spec...  6.72 us
    pallas_call x1, Pallas kernels, skeleton_solve(): pl.pallas_call(skeleton_kernel, in_specs=[pl.BlockSpec(memory_space=pltpu...  5.26 us
    ppermute x4, waiting for transfers between devices, ring(): lax.ppermute(value, axis, [(n, (n + step) % count) for n in range(count)])  5.06 us
  transfers between devices with their start and end apart: 6, of which 4 were waited for; matrix products, arithmetic and copies ran while one was open for 2% of the time, Pallas kernels for 8%

profile of v4, /device:TPU:1, one launch (start us, length us, event | category | flops | bytes accessed | tf_op | source)
XLA Modules:
  0.0 82.7 jit_solution(17799611067820382587)
XLA Ops:
  0.6 4.9 %shard_map.230 = (f32[480,128]{1,0:T(8,128)}, f32[480,128]{1,0:T(8,128)}, f32[10,32,128]{2,1,0:T(8,128)}, f32[10,32,128]{2,1,0:T(8,128)}) custom-call(f32[5,96,32,128]{3,2,1,0:T(8,128)} %refs_0_.3), custom_call_target="tpu_custom_call" | custom-call | tf_op jit(solution)/shard_map/pallas_call | solution.py:220
  5.5 2.5 %collective-permute-start = (f32[480,128]{1,0:T(8,128)}, f32[480,128]{1,0:T(8,128)}, u32[]{:S(2)}, u32[]{:S(2)}) collective-permute-start(f32[480,128]{1,0:T(8,128)} %get-tuple-element.9), channel_id=1, source_target_pairs={{0,1},{1,2},{2,3},{3,4},{4,5},{5,6},{6,7},{7,8},{8,9},{9,10},{10,1... | collective-permute-start | bytes 737288 | tf_op jit(solution)/shard_map/ppermute | solution.py:850
  8.1 4.7 %collective-permute-start.1 = (f32[480,128]{1,0:T(8,128)}, f32[480,128]{1,0:T(8,128)}, u32[]{:S(2)}, u32[]{:S(2)}) collective-permute-start(f32[480,128]{1,0:T(8,128)} %get-tuple-element.10), channel_id=1, source_target_pairs={{0,15},{1,0},{2,1},{3,2},{4,3},{5,4},{6,5},{7,6},{8,7},{9,8},{10,9... | collective-permute-start | bytes 737288 | tf_op jit(solution)/shard_map/ppermute | solution.py:850
  12.7 2.1 %collective-permute-start.2 = (f32[10,32,128]{2,1,0:T(8,128)}, f32[10,32,128]{2,1,0:T(8,128)}, u32[]{:S(2)}, u32[]{:S(2)}) collective-permute-start(f32[10,32,128]{2,1,0:T(8,128)} %get-tuple-element.11), channel_id=1, source_target_pairs={{0,16},{16,32},{32,48},{48,64},{64,80},{80,96},{96,112},{112,0},{1... | collective-permute-start | bytes 491528 | tf_op jit(solution)/shard_map/ppermute | solution.py:850
  14.8 0.0 collective-permute-start.3
  14.8 2.6 %collective-permute-done.2.refs_5_ = f32[10,32,128]{2,1,0:T(8,128)} collective-permute-done((f32[10,32,128]{2,1,0:T(8,128)}, f32[10,32,128]{2,1,0:T(8,128)}, u32[]{:S(2)}, u32[]{:S(2)}) %collective-permute-start.2) | collective-permute-done | bytes 163872 | tf_op jit(solution)/shard_map/ppermute | solution.py:850
  17.4 2.5 %collective-permute-done.3.refs_6_ = f32[10,32,128]{2,1,0:T(8,128)} collective-permute-done((f32[10,32,128]{2,1,0:T(8,128)}, f32[10,32,128]{2,1,0:T(8,128)}, u32[]{:S(2)}, u32[]{:S(2)}) %collective-permute-start.3) | collective-permute-done | bytes 163872 | tf_op jit(solution)/shard_map/ppermute | solution.py:850
  19.8 0.0 collective-permute-done.refs_3_
  19.8 0.0 collective-permute-done.1.refs_4_
  19.8 12.5 %shard_map.231 = (f32[3,96,32,128]{3,2,1,0:T(8,128)}, f32[31,96,128]{2,1,0:T(8,128)}, f32[512,128]{1,0:T(8,128)}) custom-call(f32[5,96,32,128]{3,2,1,0:T(8,128)} %refs_0_.3, s32[96,32,128]{2,1,0:T(8,128)} %refs_1_.4, s32[32,128]{1,0:T(8,128)} %refs_9_.3, f32[480,128]{1,0:T(8,128)} %collective-permute-done.refs_3_, ...), custom_call_target="tpu_custom_call" | custom-call | bytes 40000000 | tf_op jit(solution)/shard_map/pallas_call | solution.py:473
  32.3 8.9 %all-to-all-start = ((f32[128,4,128]{2,1,0:T(4,128)}), f32[128,4,128]{2,1,0:T(4,128)}, u32[]{:S(2)}, u32[]{:S(2)}) async-start(f32[128,4,128]{2,1,0:T(4,128)} %bitcast.5), calls=%async_computation | async-start | bytes 524288 | tf_op jit(solution)/shard_map/all_to_all | solution.py:855
  41.3 1.2 %dynamic_slice.3.mode_eigen = f32[1]{0:T(128)} dynamic-slice(f32[128]{0:T(128)} %constant.74.clone, s32[]{:T(128)S(6)} %select_n.3), dynamic_slice_sizes={1} | dynamic-slice | bytes 12 | tf_op jit(solution)/shard_map/dynamic_slice | solution.py:874
  42.5 9.3 %all-to-all-done = f32[128,4,128]{2,1,0:T(4,128)} async-done(((f32[128,4,128]{2,1,0:T(4,128)}), f32[128,4,128]{2,1,0:T(4,128)}, u32[]{:S(2)}, u32[]{:S(2)}) %all-to-all-start) | async-done | bytes 262176 | tf_op jit(solution)/shard_map/all_to_all | solution.py:855
  51.8 5.3 %shard_map.232 = f32[512,128]{1,0:T(8,128)} custom-call(f32[1]{0:T(128)} %dynamic_slice.3.mode_eigen, f32[512,128]{1,0:T(8,128)} %bitcast.1.refs_0_, bf16[256,256]{1,0:T(8,128)(2,1)} %constant.64.clone.refs_1_, bf16[256,256]{1,0:T(8,128)(2,1)} %constant.65.clone.refs_2_, bf16[8,256,256]{2,1,0:T(8,128)(2,1)} %constant.67.clone.refs_3_, ...), custom_call_target="tpu_custom_call" | custom-call | tf_op jit(solution)/shard_map/pallas_call | solution.py:702
  57.1 5.3 %all-to-all-start.1 = ((f32[128,4,128]{2,1,0:T(4,128)}), f32[128,4,128]{2,1,0:T(4,128)}, u32[]{:S(2)}, u32[]{:S(2)}) async-start(f32[128,4,128]{2,1,0:T(4,128)} %bitcast.4), calls=%async_computation.1 | async-start | bytes 524288 | tf_op jit(solution)/shard_map/all_to_all | solution.py:855
  62.4 6.7 %shard_map.233.refs_10_ = f32[5,96,32,128]{3,2,1,0:T(8,128)} custom-call(f32[5,96,32,128]{3,2,1,0:T(8,128)} %refs_0_.3, s32[96,32,128]{2,1,0:T(8,128)} %refs_1_.4, s32[32,128]{1,0:T(8,128)} %refs_9_.3, f32[480,128]{1,0:T(8,128)} %collective-permute-done.refs_3_, f32[480,128]{1,0:T(8,128)} %collective-permute-done.1.refs_4_, ...), custom_call_target="tpu_custom_call" | custom-call | bytes 30000000 | tf_op jit(solution)/shard_map/pallas_call | solution.py:581
  69.1 4.0 %all-to-all-done.1 = f32[128,4,128]{2,1,0:T(4,128)} async-done(((f32[128,4,128]{2,1,0:T(4,128)}), f32[128,4,128]{2,1,0:T(4,128)}, u32[]{:S(2)}, u32[]{:S(2)}) %all-to-all-start.1) | async-done | bytes 262176 | tf_op jit(solution)/shard_map/all_to_all | solution.py:855
  73.1 9.6 %shard_map.234 = (f32[5,96,32,128]{3,2,1,0:T(8,128)}, f32[96,32,128]{2,1,0:T(8,128)}) custom-call(f32[3,96,32,128]{3,2,1,0:T(8,128)} %get-tuple-element.13.refs_0_, f32[512,128]{1,0:T(8,128)} %bitcast.3.refs_1_, f32[31,96,128]{2,1,0:T(8,128)} %get-tuple-element.15.refs_2_, ...), custom_call_target="tpu_custom_call", output_to_operand_aliasing={{0}: (10, {})} | custom-call | tf_op jit(solution)/shard_map/pallas_call | solution.py:824
Async XLA Ops:
  5.5 14.3 %collective-permute-start = (f32[480,128]{1,0:T(8,128)}, f32[480,128]{1,0:T(8,128)}, u32[]{:S(2)}, u32[]{:S(2)}) collective-permute-start(f32[480,128]{1,0:T(8,128)} %get-tuple-element.9), channel_id=1, source_target_pairs={{0,1},{1,2},{2,3},{3,4},{4,5},{5,6},{6,7},{7,8},{8,9},{9,10},{10,1... | collective-permute-start | bytes 737288 | tf_op jit(solution)/shard_map/ppermute | solution.py:850
  8.1 11.8 %collective-permute-start.1 = (f32[480,128]{1,0:T(8,128)}, f32[480,128]{1,0:T(8,128)}, u32[]{:S(2)}, u32[]{:S(2)}) collective-permute-start(f32[480,128]{1,0:T(8,128)} %get-tuple-element.10), channel_id=1, source_target_pairs={{0,15},{1,0},{2,1},{3,2},{4,3},{5,4},{6,5},{7,6},{8,7},{9,8},{10,9... | collective-permute-start | bytes 737288 | tf_op jit(solution)/shard_map/ppermute | solution.py:850
  12.7 4.6 %collective-permute-start.2 = (f32[10,32,128]{2,1,0:T(8,128)}, f32[10,32,128]{2,1,0:T(8,128)}, u32[]{:S(2)}, u32[]{:S(2)}) collective-permute-start(f32[10,32,128]{2,1,0:T(8,128)} %get-tuple-element.11), channel_id=1, source_target_pairs={{0,16},{16,32},{32,48},{48,64},{64,80},{80,96},{96,112},{112,0},{1... | collective-permute-start | bytes 491528 | tf_op jit(solution)/shard_map/ppermute | solution.py:850
  14.8 5.1 %collective-permute-start.3 = (f32[10,32,128]{2,1,0:T(8,128)}, f32[10,32,128]{2,1,0:T(8,128)}, u32[]{:S(2)}, u32[]{:S(2)}) collective-permute-start(f32[10,32,128]{2,1,0:T(8,128)} %get-tuple-element.12), channel_id=1, source_target_pairs={{0,112},{16,0},{32,16},{48,32},{64,48},{80,64},{96,80},{112,96},{1... | collective-permute-start | bytes 491528 | tf_op jit(solution)/shard_map/ppermute | solution.py:850
  32.3 19.5 %all-to-all-start = ((f32[128,4,128]{2,1,0:T(4,128)}), f32[128,4,128]{2,1,0:T(4,128)}, u32[]{:S(2)}, u32[]{:S(2)}) async-start(f32[128,4,128]{2,1,0:T(4,128)} %bitcast.5), calls=%async_computation | async-start | bytes 524288 | tf_op jit(solution)/shard_map/all_to_all | solution.py:855
  57.1 16.0 %all-to-all-start.1 = ((f32[128,4,128]{2,1,0:T(4,128)}), f32[128,4,128]{2,1,0:T(4,128)}, u32[]{:S(2)}, u32[]{:S(2)}) async-start(f32[128,4,128]{2,1,0:T(4,128)} %bitcast.4), calls=%async_computation.1 | async-start | bytes 524288 | tf_op jit(solution)/shard_map/all_to_all | solution.py:855
